TPU v7x, 256 devices: a whole 4x4x8 slice. The times are simulated.
256 devices in a mesh: row: 16 (over z, core), col: 16 (over y, x).
Axes of the slice: x: 4, y: 4, z: 8, core: 2. Of those that a mesh axis runs over, the one named last changes fastest.
Arguments:
- affinity: float32 [16384, 16384], P('row', 'col'), as said below
Outputs:
- reduced: float32 [16384, 16384], P('row', 'col')
Inputs may be any that keep to these rules, and one draw needn't show every extreme that they name: The matrix that affinity stores is exactly symmetric in global indexing.
All inputs are finite; a program needn't handle non-finite values.
Results may differ from a plain program's by a relative error of at most 0.0003.
Values sent between devices are 32-bit elements; how exact they have to be, the bound alone decides.
A program may use at most 64 MiB of HBM per device.

v0:
```python
import jax
import jax.numpy as jnp
from jax import lax
from jax.sharding import PartitionSpec as P

B = 256
PANELS = 2
NS_STEPS = 12


PRECISE = lax.Precision.HIGHEST


def spread(block, axis, owner):
    block = jnp.where(lax.axis_index(axis) == owner, block, jnp.zeros_like(block))
    return lax.psum(block, axis)


def matmul(first_op, second_op, first_dim, second_dim):
    return lax.dot_general(
        first_op,
        second_op,
        (((first_dim,), (second_dim,)), ((), ())),
        precision=PRECISE,
        preferred_element_type=jnp.float32,
    )


def lower_inverse(square):
    lower_factor = jnp.linalg.cholesky(square)
    identity = jnp.eye(square.shape[0], dtype=jnp.float32)
    return lax.linalg.triangular_solve(lower_factor, identity, left_side=True, lower=True)


def reflector_parts(gram_matrix, top_block):
    inverse_low = lower_inverse(gram_matrix)
    top_basis = matmul(top_block, inverse_low, 1, 1)
    polar_part = top_basis
    for repeat in range(NS_STEPS):
        polar_part = 1.5 * polar_part - 0.5 * matmul(
            polar_part, matmul(polar_part, polar_part, 0, 0), 1, 0
        )
    cross_term = matmul(polar_part, top_basis, 0, 0)
    identity = jnp.eye(gram_matrix.shape[0], dtype=jnp.float32)
    metric = identity + cross_term + cross_term.T + matmul(polar_part, polar_part, 0, 0)
    metric_inv = lower_inverse(metric)
    middle = 2.0 * matmul(metric_inv, metric_inv, 0, 0)
    return (inverse_low, polar_part, middle)


def body(affinity):
    rows_here = affinity.shape[0]
    cols_here = affinity.shape[1]
    row_count = lax.axis_size("row")
    col_count = lax.axis_size("col")
    row_rank = lax.axis_index("row")
    col_rank = lax.axis_index("col")
    fold_count = row_count // col_count
    row_blocks = jnp.arange(rows_here, dtype=jnp.int32) // B * row_count + row_rank
    matrix = affinity

    def to_columns(row_panel):
        pieces = [spread(row_panel, "row", col_rank + 0 * col_count)]
        stacked = jnp.stack(pieces).reshape(fold_count, rows_here // B, B, B)
        return jnp.transpose(stacked, (3, 1, 0, 2)).reshape(B, cols_here)

    for panel_num in range(PANELS):
        col_start = panel_num // col_count * B
        owned_cols = matrix[:, col_start : col_start + B]
        panel_rows = spread(owned_cols, "col", panel_num % col_count)
        panel_rows = jnp.where((row_blocks > panel_num)[:, None], panel_rows, 0.0)
        top_start = (panel_num + 1) // row_count * B
        top_mask = (row_rank == (panel_num + 1) % row_count).astype(jnp.float32)
        top_piece = top_mask * panel_rows[top_start : top_start + B]
        gram_matrix, top_block = lax.psum((matmul(panel_rows, panel_rows, 0, 0), top_piece), "row")
        inverse_low, polar_part, middle = reflector_parts(gram_matrix, top_block)
        reflect_rows = (
            matmul(panel_rows, inverse_low, 1, 1)
            .at[top_start : top_start + B]
            .add(top_mask * polar_part)
        )
        reflect_cols = to_columns(reflect_rows)
        local_product = matmul(matrix, reflect_cols, 1, 1)
        product_rows = lax.psum(local_product, "col")
        image_rows = matmul(product_rows, middle, 1, 0)
        coupling = lax.psum(matmul(reflect_rows, image_rows, 0, 0), "row")
        shift_term = matmul(middle, coupling, 1, 0)
        companion_rows = image_rows - 0.5 * matmul(reflect_rows, shift_term, 1, 0)
        companion_cols = to_columns(companion_rows)
        matrix = matrix - matmul(
            jnp.concatenate((reflect_rows, companion_rows), 1),
            jnp.concatenate((companion_cols, reflect_cols), 0),
            1,
            0,
        )
    return matrix


def solution(mesh):
    return jax.shard_map(
        body,
        mesh=mesh,
        in_specs=(P("row", "col"),),
        out_specs=P("row", "col"),
        check_vma=False,
    )
```

profile of v0, /device:TPU:1, one launch (start us, length us, event | category | flops | bytes accessed | tf_op | source)
XLA Modules:
  0.0 1590.0 jit_solution(16472488823275087740)
XLA Ops:
  6.5 2.3 slice_select_fusion.1
  8.9 101.2 %all-reduce.16.cloned.1.call-done = f32[1024,256]{1,0:T(8,128)} async-done(((f32[1024,256]{1,0:T(8,128)}), f32[1024,256]{1,0:T(8,128)}) %all-reduce.16.cloned.1.call-update) | async-done | bytes 1048592 | tf_op jit(solution)/shard_map/psum | solution.py:16
  110.1 1.4 broadcast_select_fusion.1
  111.5 2.5 fusion.102
  115.1 110.6 %all-reduce.38.cloned.1.call-done = (f32[256,256]{0,1:T(8,128)}, f32[256,256]{1,0:T(8,128)}) async-done(((f32[256,256]{0,1:T(8,128)}, f32[256,256]{1,0:T(8,128)}), (f32[256,256]{0,1:T(8,128)}, f32[256,256]{1,0:T(8,128)})) %all-reduce.38.cloned.1.call-update) | async-done | bytes 524304 | tf_op jit(solution)/shard_map/psum | solution.py:75
  227.8 11.7 cholesky.214
  239.5 9.8 custom-call.17
  249.8 11.7 cholesky.231
  263.6 3.9 while.10
  267.6 20.1 %custom-call.18 = f32[2,128,128]{1,2,0:T(8,128)S(1)} custom-call(f32[2,128,128]{2,1,0:T(8,128)S(1)} %get-tuple-element.57), custom_call_target="InvertDiagBlocksLowerTriangular" | custom-call | tf_op jit(solution)/shard_map/triangular_solve/custom-call.0 | solution.py:32
  303.9 11.7 cholesky.248
  316.3 9.8 custom-call.19
  326.6 11.9 cholesky.265
  341.6 109.7 %all-reduce.18.cloned.1.call-done = f32[256,1024]{0,1:T(8,128)} async-done(((f32[256,1024]{0,1:T(8,128)}), f32[256,1024]{0,1:T(8,128)}) %all-reduce.18.cloned.1.call-update) | async-done | bytes 1048592 | tf_op jit(solution)/shard_map/psum | solution.py:16
  451.3 10.3 convolution_bitcast_fusion
  461.7 4.2 while.11
  465.9 19.7 %custom-call.20 = f32[2,128,128]{1,2,0:T(8,128)S(1)} custom-call(f32[2,128,128]{2,1,0:T(8,128)S(1)} %get-tuple-element.58), custom_call_target="InvertDiagBlocksLowerTriangular" | custom-call | tf_op jit(solution)/shard_map/triangular_solve/custom-call.0 | solution.py:32
  487.2 70.8 %all-reduce.20.cloned.1.call-done = f32[1024,256]{0,1:T(8,128)} async-done(((f32[1024,256]{0,1:T(8,128)}), f32[1024,256]{0,1:T(8,128)}) %all-reduce.20.cloned.1.call-update) | async-done | bytes 1048592 | tf_op jit(solution)/shard_map/psum | solution.py:84
  558.0 3.0 fusion.116
  561.0 2.5 fusion.117
  563.6 109.4 %all-reduce.22.cloned.1.call-done = f32[256,256]{1,0:T(8,128)} async-done(((f32[256,256]{1,0:T(8,128)}), f32[256,256]{1,0:T(8,128)}) %all-reduce.22.cloned.1.call-update) | async-done | bytes 262160 | tf_op jit(solution)/shard_map/psum | solution.py:86
  676.5 111.7 %all-reduce.24.cloned.1.call-done = f32[256,1024]{0,1:T(8,128)} async-done(((f32[256,1024]{0,1:T(8,128)}), f32[256,1024]{0,1:T(8,128)}) %all-reduce.24.cloned.1.call-update) | async-done | bytes 1048592 | tf_op jit(solution)/shard_map/psum | solution.py:16
  788.1 10.3 convolution_subtract_fusion.1
  798.4 2.0 copy-done
  801.7 96.2 %all-reduce.26.cloned.1.call-done = f32[1024,256]{1,0:T(8,128)} async-done(((f32[1024,256]{1,0:T(8,128)}), f32[1024,256]{1,0:T(8,128)}) %all-reduce.26.cloned.1.call-update) | async-done | bytes 1048592 | tf_op jit(solution)/shard_map/psum | solution.py:16
  897.9 1.4 broadcast_select_fusion
  899.3 2.5 fusion.119
  902.8 110.6 %all-reduce.36.cloned.1.call-done = (f32[256,256]{0,1:T(8,128)}, f32[256,256]{1,0:T(8,128)}) async-done(((f32[256,256]{0,1:T(8,128)}, f32[256,256]{1,0:T(8,128)}), (f32[256,256]{0,1:T(8,128)}, f32[256,256]{1,0:T(8,128)})) %all-reduce.36.cloned.1.call-update) | async-done | bytes 524304 | tf_op jit(solution)/shard_map/psum | solution.py:75
  1015.5 11.7 cholesky.282
  1028.0 9.8 custom-call.21
  1038.3 11.7 cholesky.299
  1052.0 4.0 while.12
  1056.1 20.1 %custom-call.22 = f32[2,128,128]{1,2,0:T(8,128)S(1)} custom-call(f32[2,128,128]{2,1,0:T(8,128)S(1)} %get-tuple-element.59), custom_call_target="InvertDiagBlocksLowerTriangular" | custom-call | tf_op jit(solution)/shard_map/triangular_solve/custom-call.0 | solution.py:32
  1092.4 11.7 cholesky.316
  1104.8 9.8 custom-call.23
  1115.1 11.9 cholesky.333
  1130.2 109.9 %all-reduce.28.cloned.1.call-done = f32[256,1024]{0,1:T(8,128)} async-done(((f32[256,1024]{0,1:T(8,128)}), f32[256,1024]{0,1:T(8,128)}) %all-reduce.28.cloned.1.call-update) | async-done | bytes 1048592 | tf_op jit(solution)/shard_map/psum | solution.py:16
  1240.1 6.9 fusion.132
  1247.0 4.1 while.13
  1247.7 1.4 bitcast_dynamic-update-slice_fusion.11
  1249.7 1.4 bitcast_dynamic-update-slice_fusion.11
  1251.1 19.7 %custom-call.24 = f32[2,128,128]{1,2,0:T(8,128)S(1)} custom-call(f32[2,128,128]{2,1,0:T(8,128)S(1)} %get-tuple-element.60), custom_call_target="InvertDiagBlocksLowerTriangular" | custom-call | tf_op jit(solution)/shard_map/triangular_solve/custom-call.0 | solution.py:32
  1272.4 70.9 %all-reduce.30.cloned.1.call-done = f32[1024,256]{1,0:T(8,128)} async-done(((f32[1024,256]{1,0:T(8,128)}), f32[1024,256]{1,0:T(8,128)}) %all-reduce.30.cloned.1.call-update) | async-done | bytes 1048592 | tf_op jit(solution)/shard_map/psum | solution.py:84
  1343.3 2.2 fusion.134
  1345.5 2.5 fusion.135
  1348.4 109.1 %all-reduce.32.cloned.1.call-done = f32[256,256]{1,0:T(8,128)} async-done(((f32[256,256]{1,0:T(8,128)}), f32[256,256]{1,0:T(8,128)}) %all-reduce.32.cloned.1.call-update) | async-done | bytes 262160 | tf_op jit(solution)/shard_map/psum | solution.py:86
  1461.0 111.7 %all-reduce.34.cloned.1.call-done = f32[256,1024]{0,1:T(8,128)} async-done(((f32[256,1024]{0,1:T(8,128)}), f32[256,1024]{0,1:T(8,128)}) %all-reduce.34.cloned.1.call-update) | async-done | bytes 1048592 | tf_op jit(solution)/shard_map/psum | solution.py:16
  1572.7 10.2 convolution_subtract_fusion
  (186 shorter events, 72.2 us)
Async XLA Ops:
  6.5 103.6 %all-reduce.16.cloned.1.call-start = ((), (), s32[]{:S(2)}) async-start(), calls=%async_computation | async-start | bytes 2097152 | tf_op jit(solution)/shard_map/psum | solution.py:16
  8.9 216.8 %all-reduce.38.cloned.1.call-start = ((), (), s32[]{:S(2)}) async-start(), calls=%async_computation.11 | async-start | bytes 1048576 | tf_op jit(solution)/shard_map/psum | solution.py:75
  114.8 336.5 %all-reduce.18.cloned.1.call-start = ((), (), s32[]{:S(2)}) async-start(), calls=%async_computation.1 | async-start | bytes 2097152 | tf_op jit(solution)/shard_map/psum | solution.py:16
  225.6 64.1 %copy-start.1 = (f32[256,256]{1,0:T(8,128)S(1)}, f32[256,256]{1,0:T(8,128)}, u32[]{:S(2)}) copy-start(f32[256,256]{1,0:T(8,128)} %get-tuple-element.96) | copy-start | bytes 786436
  339.6 218.4 %all-reduce.20.cloned.1.call-start = ((), (), s32[]{:S(2)}) async-start(), calls=%async_computation.2 | async-start | bytes 2097152 | tf_op jit(solution)/shard_map/psum | solution.py:84
  461.6 211.4 %all-reduce.22.cloned.1.call-start = ((), (), s32[]{:S(2)}) async-start(), calls=%async_computation.3 | async-start | bytes 524288 | tf_op jit(solution)/shard_map/psum | solution.py:86
  563.6 224.5 %all-reduce.24.cloned.1.call-start = ((), (), s32[]{:S(2)}) async-start(), calls=%async_computation.4 | async-start | bytes 2097152 | tf_op jit(solution)/shard_map/psum | solution.py:16
  676.4 221.5 %all-reduce.26.cloned.1.call-start = ((), (), s32[]{:S(2)}) async-start(), calls=%async_computation.5 | async-start | bytes 2097152 | tf_op jit(solution)/shard_map/psum | solution.py:16
  798.4 2.0 copy-start
  801.6 211.8 %all-reduce.36.cloned.1.call-start = ((), (), s32[]{:S(2)}) async-start(), calls=%async_computation.10 | async-start | bytes 1048576 | tf_op jit(solution)/shard_map/psum | solution.py:75
  902.6 337.5 %all-reduce.28.cloned.1.call-start = ((), (), s32[]{:S(2)}) async-start(), calls=%async_computation.6 | async-start | bytes 2097152 | tf_op jit(solution)/shard_map/psum | solution.py:16
  1013.4 64.8 %copy-start.2 = (f32[256,256]{1,0:T(8,128)S(1)}, f32[256,256]{1,0:T(8,128)}, u32[]{:S(2)}) copy-start(f32[256,256]{1,0:T(8,128)} %get-tuple-element.94) | copy-start | bytes 786436
  1128.2 215.2 %all-reduce.30.cloned.1.call-start = ((), (), s32[]{:S(2)}) async-start(), calls=%async_computation.7 | async-start | bytes 2097152 | tf_op jit(solution)/shard_map/psum | solution.py:84
  1247.0 210.6 %all-reduce.32.cloned.1.call-start = ((), (), s32[]{:S(2)}) async-start(), calls=%async_computation.8 | async-start | bytes 524288 | tf_op jit(solution)/shard_map/psum | solution.py:86
  1348.1 224.5 %all-reduce.34.cloned.1.call-start = ((), (), s32[]{:S(2)}) async-start(), calls=%async_computation.9 | async-start | bytes 2097152 | tf_op jit(solution)/shard_map/psum | solution.py:16
Sparse Core Ops, SparseCore 0:
  10.6 99.4 all-reduce.15
  114.9 110.6 all-reduce.37
  339.7 111.5 all-reduce.17
  461.7 96.2 all-reduce.19
  563.7 109.2 all-reduce.21
  676.5 111.5 all-reduce.23
  801.8 96.0 all-reduce.25
  902.7 110.6 all-reduce.35
  1128.3 111.7 all-reduce.27
  1247.1 96.2 all-reduce.29
  1348.2 109.2 all-reduce.31
  1461.1 111.5 all-reduce.33
where the time goes:
time: 1590 us
  waiting for transfers between devices  1220 us (77%)
  other arithmetic  232 us (15%)
  matrix products  94 us (6%)
  local copies, waits for them, and re-layouts  20.8 us (1%)
  between operations  19.9 us (1%)
    psum x6, waiting for transfers between devices, spread(): return lax.psum(block, axis)  640 us
    psum x2, waiting for transfers between devices, body(): lax.psum((matmul(panel_rows, panel_rows, 0, 0), top_piece), 'row')  221 us
    psum x2, waiting for transfers between devices, body(): coupling = lax.psum(matmul(reflect_rows, image_rows, 0, 0), 'row')  218 us
    psum x2, waiting for transfers between devices, body(): product_rows = lax.psum(local_product, 'col')  142 us
    another operation x27, other arithmetic, lower_inverse(): lower_factor = jnp.linalg.cholesky(square)  138 us
    dot_general x72, matrix products, matmul(): lax.dot_general(first_op, second_op, (((first_dim,), (second_dim,)), ((),...  88.1 us
    another operation x9, other arithmetic, lower_inverse(): lax.linalg.triangular_solve(lower_factor, identity, left_side=True, lower...  79.6 us
  transfers between devices with their start and end apart: 12, of which 12 were waited for; matrix products, arithmetic and copies ran while one was open for 3% of the time, Pallas kernels for 0%

commit v1 on v0

v1 whole, which is shorter than its diff:
```python
import functools

import jax
import jax.numpy as jnp
from jax import lax
from jax.experimental import pallas as pl
from jax.experimental.pallas import tpu as pltpu
from jax.sharding import PartitionSpec as P

B = 256
PANELS = 2
NS_STEPS = 12
D = 16
PIECE = 64
SLICE = 16
MESH = pl.DeviceIdType.MESH
HIGHEST = lax.Precision.HIGHEST
VMEM_LIMIT = 56 * 1024 * 1024


def dot(first, second, first_dim, second_dim):
    return lax.dot_general(
        first,
        second,
        (((first_dim,), (second_dim,)), ((), ())),
        precision=HIGHEST,
        preferred_element_type=jnp.float32,
    )


def split(value):
    high = value.astype(jnp.bfloat16)
    return high, (value - high.astype(jnp.float32)).astype(jnp.bfloat16)


def dot_split(first, second, first_dim, second_dim):
    def one(x, y):
        return lax.dot_general(
            x, y, (((first_dim,), (second_dim,)), ((), ())), preferred_element_type=jnp.float32
        )

    return one(first[0], second[0]) + (one(first[0], second[1]) + one(first[1], second[0]))


def dot3(first, second, first_dim, second_dim):
    return dot_split(split(first), split(second), first_dim, second_dim)


def sublane(x, j):
    return jnp.broadcast_to(x[j : j + 1, :], x.shape)


def chol_inverse_128(d_ref):
    n = 128
    sub = lax.broadcasted_iota(jnp.int32, (8, n), 0)
    lane = lax.broadcasted_iota(jnp.int32, (8, n), 1)
    rows = [d_ref[8 * g : 8 * g + 8, :] for g in range(n // 8)]
    for g in range(n // 8):
        k0 = 8 * g
        own = (lane >= k0) & (lane < k0 + 8)
        unit = jnp.where(lane == sub + k0, 1.0, 0.0)
        cur = rows[g]
        cols = [jnp.broadcast_to(cur[:, k0 + j : k0 + j + 1], (8, n)) for j in range(8)]
        cur = jnp.where(own, unit, cur)
        recips, factors, pivots = [], {}, []
        diag = jnp.ones((8, n), jnp.float32)
        for j in range(8):
            d = sublane(cols[j], j)
            recips.append(1.0 / d)
            diag = jnp.where(sub == j, d, diag)
            f = jnp.where(sub > j, cols[j] * recips[j], 0.0)
            for l in range(j + 1, 8):
                factors[j, l] = sublane(cols[l], j)
                cols[l] = cols[l] - f * factors[j, l]
            pivots.append(sublane(cur, j))
            cur = cur - f * pivots[j]
        d_ref[k0 : k0 + 8, :] = jnp.where(lane < k0 + 8, cur, 0.0) / jnp.sqrt(diag)
        for i in range(g + 1, n // 8):
            low = rows[i]
            cols = [jnp.broadcast_to(low[:, k0 + j : k0 + j + 1], (8, n)) for j in range(8)]
            low = jnp.where(own, 0.0, low)
            for j in range(8):
                f = cols[j] * recips[j]
                for l in range(j + 1, 8):
                    cols[l] = cols[l] - f * factors[j, l]
                low = low - f * pivots[j]
            rows[i] = low


def chol_inverse(gram, out_ref, d_ref):
    half = B // 2
    d_ref[...] = gram[:half, :half]
    chol_inverse_128(d_ref)
    first = d_ref[...]
    below = dot(gram[half:, :half], first, 1, 1)
    d_ref[...] = gram[half:, half:] - dot(below, below, 1, 1)
    chol_inverse_128(d_ref)
    second = d_ref[...]
    out_ref[:half, :half] = first
    out_ref[:half, half:] = jnp.zeros((half, half), jnp.float32)
    out_ref[half:, :half] = -dot(second, dot(below, first, 1, 0), 1, 0)
    out_ref[half:, half:] = second


def eye():
    r = lax.broadcasted_iota(jnp.int32, (B, B), 0)
    c = lax.broadcasted_iota(jnp.int32, (B, B), 1)
    return jnp.where(r == c, 1.0, 0.0)


def factor_kernel(
    panel, a_ref, pr_ref, pq_ref, gt_ref,
    vr_ref, vq_ref, mid_ref, x_ref, kp_ref,
    inv_ref, d_ref, w_ref,
):
    p, q = lax.axis_index("row"), lax.axis_index("col")
    gt = gt_ref[...]
    gram = gt[:, :SLICE, :].reshape(B, B)
    block = gt[:, SLICE:, :].reshape(B, B)
    chol_inverse(gram, inv_ref, d_ref)
    inverse_low = inv_ref[...]
    top = dot(block, inverse_low, 1, 1)
    w_ref[...] = top

    def step(i, carry):
        w = w_ref[...]
        s = split(w)
        w_ref[...] = 1.5 * w - 0.5 * dot_split(s, split(dot_split(s, s, 0, 0)), 1, 0)
        return carry

    lax.fori_loop(0, NS_STEPS, step, 0)
    w = w_ref[...]
    cross = dot(w, top, 0, 0)
    metric = eye() + cross + cross.T + dot(w, w, 0, 0)
    guess = (40.0 / 41.0) * eye() - (8.0 / 41.0) * metric
    for i in range(4):
        mul = dot if i == 3 else dot3
        guess = guess + mul(guess, eye() - mul(metric, guess, 1, 0), 1, 0)
    mid_ref[...] = 2.0 * guess

    inv_split = split(inverse_low)
    for tile in range(4):
        rows = slice(tile * B, tile * B + B)
        vr_ref[rows, :] = dot_split(split(pr_ref[rows, :]), inv_split, 1, 1)
        vq_ref[rows, :] = dot_split(split(pq_ref[rows, :]), inv_split, 1, 1)
    here = jnp.where(p == panel + 1, 1.0, 0.0)
    vr_ref[:B, :] = vr_ref[:B, :] + here * w
    here = jnp.where(q == panel + 1, 1.0, 0.0)
    vq_ref[:B, :] = vq_ref[:B, :] + here * w

    vq = split(vq_ref[...])
    kp_ref[...] = jnp.zeros((B, B), jnp.float32)

    def tile_step(tile, carry):
        rows = pl.ds(pl.multiple_of(tile * B, B), B)
        x = dot_split(split(a_ref[rows, :]), vq, 1, 0)
        x_ref[rows, :] = x
        kp_ref[...] += dot3(vr_ref[rows, :], x, 0, 0)
        return carry

    lax.fori_loop(0, 4, tile_step, 0)


def factor(panel, matrix, pr, pq, gt):
    vmem = pl.BlockSpec(memory_space=pltpu.VMEM)
    tall = jax.ShapeDtypeStruct((4 * B, B), jnp.float32)
    square = jax.ShapeDtypeStruct((B, B), jnp.float32)
    return pl.pallas_call(
        functools.partial(factor_kernel, panel),
        out_shape=(tall, tall, square, tall, square),
        in_specs=[vmem] * 4,
        out_specs=(vmem,) * 5,
        scratch_shapes=[
            pltpu.VMEM((B, B), jnp.float32),
            pltpu.VMEM((B // 2, B // 2), jnp.float32),
            pltpu.VMEM((B, B), jnp.float32),
        ],
        compiler_params=pltpu.CompilerParams(vmem_limit_bytes=VMEM_LIMIT),
        name=f"factor_{panel}",
    )(matrix, pr, pq, gt)


def greet(p, q, partner):
    barrier = pltpu.get_barrier_semaphore()
    for i in range(1, D):
        pl.semaphore_signal(
            barrier, inc=1, device_id=(lax.rem(p + i, D), q), device_id_type=MESH
        )
        pl.semaphore_signal(
            barrier, inc=1, device_id=(p, lax.rem(q + i, D)), device_id_type=MESH
        )
    if partner:

        @pl.when(p != q)
        def _():
            pl.semaphore_signal(barrier, inc=1, device_id=(q, p), device_id_type=MESH)
            pl.semaphore_wait(barrier, 2 * (D - 1) + 1)

        @pl.when(p == q)
        def _():
            pl.semaphore_wait(barrier, 2 * (D - 1))

    else:
        pl.semaphore_wait(barrier, 2 * (D - 1))


def remote(src, dst, send, recv, target):
    return pltpu.make_async_remote_copy(
        src_ref=src, dst_ref=dst, send_sem=send, recv_sem=recv,
        device_id=target, device_id_type=MESH,
    )


def piece(index):
    return pl.ds(pl.multiple_of(index * PIECE, PIECE), PIECE)


def slab(index):
    return pl.ds(pl.multiple_of(index * SLICE, SLICE), SLICE)


def gather_col_start(ref, at, send, recv, p, q):
    for i in range(1, D):
        t = lax.rem(q + i, D)
        remote(ref.at[at(q)], ref.at[at(q)], send.at[i], recv.at[q], (p, t)).start()


def gather_col_wait(ref, at, send, recv, p, q):
    for i in range(1, D):
        t = lax.rem(q + i, D)
        remote(ref.at[at(t)], ref.at[at(t)], send.at[i], recv.at[t], (p, t)).wait_recv()


def gather_col_drain(ref, at, send, recv, p, q):
    for i in range(1, D):
        t = lax.rem(q + i, D)
        remote(ref.at[at(q)], ref.at[at(q)], send.at[i], recv.at[q], (p, t)).wait_send()


def gather_row_start(ref, send, recv, p, q):
    for i in range(0, D, 2):
        t = lax.rem(p + i, D) if i else p + 1 - 2 * lax.rem(p, 2)
        remote(ref.at[piece(p)], ref.at[piece(p)], send.at[i], recv.at[p], (t, q)).start()


def gather_row_pass(ref, send, recv, p, q):
    other = p + 1 - 2 * lax.rem(p, 2)
    for i in (2, 14, 4, 12, 6, 10, 8):
        t = lax.rem(p + i, D)
        remote(ref.at[piece(t)], ref.at[piece(t)], send.at[i], recv.at[t], (t, q)).wait_recv()
        remote(ref.at[piece(t)], ref.at[piece(t)], send.at[i + 1], recv.at[t], (other, q)).start()


def gather_row_wait(ref, send, recv, p, q):
    other = p + 1 - 2 * lax.rem(p, 2)
    for i in range(0, D, 2):
        t = lax.rem(other + i, D)
        remote(ref.at[piece(t)], ref.at[piece(t)], send.at[i], recv.at[t], (other, q)).wait_recv()


def gather_row_drain(ref, send, recv, p, q):
    other = p + 1 - 2 * lax.rem(p, 2)
    for i in range(0, D, 2):
        remote(ref.at[piece(p)], ref.at[piece(p)], send.at[i], recv.at[p], (other, q)).wait_send()
        if i:
            t = lax.rem(p + i, D)
            remote(
                ref.at[piece(t)], ref.at[piece(t)], send.at[i + 1], recv.at[t], (other, q)
            ).wait_send()


def panel_kernel(
    panel, a_ref, pr_ref, pq_ref, gt_ref,
    tall, wide, turned, gram, part, block,
    load, gram_s, gram_r, block_s, block_r, down_s, down_r, gt_s, gt_r,
    prs_s, prs_r, pr_s, pr_r, pqs_s, pqs_r, pq_s, pq_r,
):
    p, q = lax.axis_index("row"), lax.axis_index("col")
    greet(p, q, False)
    row_owner, col_owner = p == panel, q == panel
    whole = lambda index: index
    load_tall = pltpu.make_async_copy(a_ref.at[:, pl.ds(0, B)], tall, load.at[0])
    load_wide = pltpu.make_async_copy(a_ref.at[pl.ds(0, B), :], wide, load.at[1])

    @pl.when(col_owner)
    def _():
        load_tall.start()

    @pl.when(row_owner)
    def _():
        load_wide.start()
        load_wide.wait()

        @pl.when(q <= panel)
        def _():
            wide[:, :B] = jnp.zeros((B, B), jnp.float32)

        gram[...] = dot(wide[...], wide[...], 1, 1)
        for i in range(1, D):
            t = lax.rem(q + i, D)
            remote(gram.at[slab(t)], part.at[q], gram_s.at[i], gram_r.at[q], (p, t)).start()
        part[q] = gram[slab(q), :]

        @pl.when(q == panel + 1)
        def _():
            block[...] = wide[:, :B].T
            for i in range(1, D):
                t = lax.rem(q + i, D)
                remote(
                    block.at[slab(t)], gt_ref.at[t, pl.ds(SLICE, SLICE)],
                    block_s.at[i], block_r, (p, t),
                ).start()
            gt_ref[q, SLICE:, :] = block[slab(q), :]

        turned[...] = wide[...].T
        for i in range(1, D):
            t = lax.rem(p + i, D)
            remote(
                turned.at[piece(t)], pq_ref.at[piece(t)], pqs_s.at[i], pqs_r, (t, q)
            ).start()
        pq_ref[piece(p), :] = turned[piece(p), :]

    @pl.when(col_owner)
    def _():
        load_tall.wait()

        @pl.when(p <= panel)
        def _():
            tall[:B, :] = jnp.zeros((B, B), jnp.float32)

        for i in range(1, D):
            t = lax.rem(q + i, D)
            remote(tall.at[piece(t)], pr_ref.at[piece(t)], prs_s.at[i], prs_r, (p, t)).start()
        pr_ref[piece(q), :] = tall[piece(q), :]

    @pl.when(row_owner)
    def _():
        for i in range(1, D):
            t = lax.rem(q + i, D)
            remote(gram.at[slab(q)], part.at[t], gram_s.at[i], gram_r.at[t], (p, t)).wait_recv()
        total = part[0]
        for i in range(1, D):
            total = total + part[i]
        gt_ref[q, :SLICE, :] = total

        @pl.when(q != panel + 1)
        def _():
            remote(
                block.at[slab(q)], gt_ref.at[q, pl.ds(SLICE, SLICE)], block_s.at[0], block_r, (p, q)
            ).wait_recv()

        for i in range(1, D):
            t = lax.rem(p + i, D)
            remote(gt_ref.at[q], gt_ref.at[q], down_s.at[i], down_r, (t, q)).start()

    @pl.when(jnp.logical_not(row_owner))
    def _():
        remote(turned.at[piece(p)], pq_ref.at[piece(p)], pqs_s.at[0], pqs_r, (p, q)).wait_recv()

    gather_row_start(pq_ref, pq_s, pq_r, p, q)

    @pl.when(jnp.logical_not(col_owner))
    def _():
        remote(tall.at[piece(q)], pr_ref.at[piece(q)], prs_s.at[0], prs_r, (p, q)).wait_recv()

    gather_col_start(pr_ref, piece, pr_s, pr_r, p, q)

    @pl.when(jnp.logical_not(row_owner))
    def _():
        remote(gt_ref.at[q], gt_ref.at[q], down_s.at[0], down_r, (p, q)).wait_recv()

    gather_col_start(gt_ref, whole, gt_s, gt_r, p, q)
    gather_row_pass(pq_ref, pq_s, pq_r, p, q)
    gather_col_wait(pr_ref, piece, pr_s, pr_r, p, q)
    gather_col_wait(gt_ref, whole, gt_s, gt_r, p, q)
    gather_row_wait(pq_ref, pq_s, pq_r, p, q)
    gather_row_drain(pq_ref, pq_s, pq_r, p, q)
    gather_col_drain(pr_ref, piece, pr_s, pr_r, p, q)
    gather_col_drain(gt_ref, whole, gt_s, gt_r, p, q)

    @pl.when(row_owner)
    def _():
        for i in range(1, D):
            t = lax.rem(q + i, D)
            remote(gram.at[slab(t)], part.at[q], gram_s.at[i], gram_r.at[q], (p, t)).wait_send()
            t = lax.rem(p + i, D)
            remote(
                turned.at[piece(t)], pq_ref.at[piece(t)], pqs_s.at[i], pqs_r, (t, q)
            ).wait_send()
            remote(gt_ref.at[q], gt_ref.at[q], down_s.at[i], down_r, (t, q)).wait_send()

        @pl.when(q == panel + 1)
        def _():
            for i in range(1, D):
                t = lax.rem(q + i, D)
                remote(
                    block.at[slab(t)], gt_ref.at[t, pl.ds(SLICE, SLICE)],
                    block_s.at[i], block_r, (p, t),
                ).wait_send()

    @pl.when(col_owner)
    def _():
        for i in range(1, D):
            t = lax.rem(q + i, D)
            remote(tall.at[piece(t)], pr_ref.at[piece(t)], prs_s.at[i], prs_r, (p, t)).wait_send()


def share_panel(panel, matrix):
    vmem = pl.BlockSpec(memory_space=pltpu.VMEM)
    tall = jax.ShapeDtypeStruct((4 * B, B), jnp.float32)
    many, one = pltpu.SemaphoreType.DMA((D,)), pltpu.SemaphoreType.DMA
    return pl.pallas_call(
        functools.partial(panel_kernel, panel),
        out_shape=(tall, tall, jax.ShapeDtypeStruct((D, 2 * SLICE, B), jnp.float32)),
        in_specs=[pl.BlockSpec(memory_space=pl.ANY)],
        out_specs=(vmem,) * 3,
        scratch_shapes=[
            pltpu.VMEM((4 * B, B), jnp.float32),
            pltpu.VMEM((B, 4 * B), jnp.float32),
            pltpu.VMEM((4 * B, B), jnp.float32),
            pltpu.VMEM((B, B), jnp.float32),
            pltpu.VMEM((D, SLICE, B), jnp.float32),
            pltpu.VMEM((B, B), jnp.float32),
            pltpu.SemaphoreType.DMA((2,)),
            many, many, many, one, many, one, many, many,
            many, one, many, many, many, one, many, many,
        ],
        compiler_params=pltpu.CompilerParams(
            collective_id=1 + panel, has_side_effects=True, vmem_limit_bytes=VMEM_LIMIT
        ),
        name=f"share_panel_{panel}",
    )(matrix)


def image_kernel(
    x_ref, kp_ref, mid_ref, cp_ref, cq_ref, k_ref,
    parts, kparts, ksum, krows,
    x_s, x_r, kp_s, kp_r, kr_s, kr_r, k_s, k_r, cp_s, cp_r, turn_s, turn_r, cq_s, cq_r,
):
    p, q = lax.axis_index("row"), lax.axis_index("col")
    greet(p, q, True)
    for i in range(1, D):
        t = lax.rem(q + i, D)
        remote(kp_ref.at[slab(t)], kparts.at[q], kp_s.at[i], kp_r.at[q], (p, t)).start()
    for i in range(1, D):
        t = lax.rem(q + i, D)
        remote(x_ref.at[piece(t)], parts.at[q], x_s.at[i], x_r.at[q], (p, t)).start()
    kparts[q] = kp_ref[slab(q), :]
    parts[q] = x_ref[piece(q), :]

    for i in range(1, D):
        t = lax.rem(q + i, D)
        remote(kp_ref.at[slab(q)], kparts.at[t], kp_s.at[i], kp_r.at[t], (p, t)).wait_recv()
    total = kparts[0]
    for i in range(1, D):
        total = total + kparts[i]
    ksum[...] = total
    krows[p] = total
    for i in range(1, D):
        t = lax.rem(p + i, D)
        remote(ksum, krows.at[p], kr_s.at[i], kr_r.at[p], (t, q)).start()

    for i in range(1, D):
        t = lax.rem(q + i, D)
        remote(x_ref.at[piece(q)], parts.at[t], x_s.at[i], x_r.at[t], (p, t)).wait_recv()
    total = parts[0]
    for i in range(1, D):
        total = total + parts[i]
    image = dot(total, mid_ref[...], 1, 0)
    cp_ref[piece(q), :] = image

    @pl.when(p != q)
    def _():
        remote(cp_ref.at[piece(q)], cq_ref.at[piece(q)], turn_s, turn_r, (q, p)).start()

    @pl.when(p == q)
    def _():
        cq_ref[piece(p), :] = image

    gather_col_start(cp_ref, piece, cp_s, cp_r, p, q)

    for i in range(1, D):
        t = lax.rem(p + i, D)
        remote(ksum, krows.at[t], kr_s.at[i], kr_r.at[t], (t, q)).wait_recv()
    total = krows[0]
    for i in range(1, D):
        total = total + krows[i]
    k_ref[slab(q), :] = total
    gather_col_start(k_ref, slab, k_s, k_r, p, q)

    @pl.when(p != q)
    def _():
        remote(cp_ref.at[piece(q)], cq_ref.at[piece(p)], turn_s, turn_r, (q, p)).wait_recv()

    gather_row_start(cq_ref, cq_s, cq_r, p, q)
    gather_row_pass(cq_ref, cq_s, cq_r, p, q)
    gather_col_wait(cp_ref, piece, cp_s, cp_r, p, q)
    gather_col_wait(k_ref, slab, k_s, k_r, p, q)
    gather_row_wait(cq_ref, cq_s, cq_r, p, q)

    gather_row_drain(cq_ref, cq_s, cq_r, p, q)
    gather_col_drain(cp_ref, piece, cp_s, cp_r, p, q)
    gather_col_drain(k_ref, slab, k_s, k_r, p, q)

    @pl.when(p != q)
    def _():
        remote(cp_ref.at[piece(q)], cq_ref.at[piece(q)], turn_s, turn_r, (q, p)).wait_send()

    for i in range(1, D):
        t = lax.rem(q + i, D)
        remote(kp_ref.at[slab(t)], kparts.at[q], kp_s.at[i], kp_r.at[q], (p, t)).wait_send()
        remote(x_ref.at[piece(t)], parts.at[q], x_s.at[i], x_r.at[q], (p, t)).wait_send()
        t = lax.rem(p + i, D)
        remote(ksum, krows.at[p], kr_s.at[i], kr_r.at[p], (t, q)).wait_send()


def share_image(x, kp, middle):
    vmem = pl.BlockSpec(memory_space=pltpu.VMEM)
    tall = jax.ShapeDtypeStruct((4 * B, B), jnp.float32)
    many, one = pltpu.SemaphoreType.DMA((D,)), pltpu.SemaphoreType.DMA
    return pl.pallas_call(
        image_kernel,
        out_shape=(tall, tall, jax.ShapeDtypeStruct((B, B), jnp.float32)),
        in_specs=[vmem] * 3,
        out_specs=(vmem,) * 3,
        scratch_shapes=[
            pltpu.VMEM((D, PIECE, B), jnp.float32),
            pltpu.VMEM((D, SLICE, B), jnp.float32),
            pltpu.VMEM((SLICE, B), jnp.float32),
            pltpu.VMEM((D, SLICE, B), jnp.float32),
            many, many, many, many, many, many, many, many, many, many, one, one, many, many,
        ],
        compiler_params=pltpu.CompilerParams(
            collective_id=8, has_side_effects=True, vmem_limit_bytes=VMEM_LIMIT
        ),
        name="share_image",
    )(x, kp, middle)


def update_kernel(
    a_ref, vr_ref, cp_ref, vq_ref, cq_ref, k_ref, mid_ref, out_ref, right_high, right_low
):
    @pl.when(pl.program_id(0) == 0)
    def _():
        middle = mid_ref[...]
        shift = dot3(dot3(middle, k_ref[...], 1, 0), middle, 1, 0)
        shift = split(0.5 * (shift + shift.T))
        for tile in range(4):
            rows = slice(tile * B, tile * B + B)
            vq = vq_ref[rows, :]
            high, low = split(vq.T)
            right_high[:B, rows] = high
            right_low[:B, rows] = low
            other = cq_ref[rows, :] - dot_split(split(vq), shift, 1, 0)
            high, low = split(other.T)
            right_high[B:, rows] = high
            right_low[B:, rows] = low

    left = split(jnp.concatenate((cp_ref[...], vr_ref[...]), 1))
    out_ref[...] = a_ref[...] - dot_split(left, (right_high[...], right_low[...]), 1, 0)


def update(matrix, vr, cp, vq, cq, k, middle):
    rows = 128
    size = 4 * B
    whole = lambda shape: pl.BlockSpec(shape, lambda i: (0, 0))
    tile = lambda width: pl.BlockSpec((rows, width), lambda i: (i, 0))
    return pl.pallas_call(
        update_kernel,
        out_shape=jax.ShapeDtypeStruct((size, size), jnp.float32),
        grid=(size // rows,),
        in_specs=[
            tile(size), tile(B), tile(B), whole((size, B)), whole((size, B)),
            whole((B, B)), whole((B, B)),
        ],
        out_specs=tile(size),
        scratch_shapes=[pltpu.VMEM((2 * B, size), jnp.bfloat16)] * 2,
        compiler_params=pltpu.CompilerParams(vmem_limit_bytes=VMEM_LIMIT),
        name="update",
    )(matrix, vr, cp, vq, cq, k, middle)


def body(affinity):
    matrix = affinity
    for panel in range(PANELS):
        pr, pq, gt = share_panel(panel, matrix)
        vr, vq, middle, x, kp = factor(panel, matrix, pr, pq, gt)
        cp, cq, k = share_image(x, kp, middle)
        matrix = update(matrix, vr, cp, vq, cq, k, middle)
    return matrix


def solution(mesh):
    return jax.shard_map(
        body,
        mesh=mesh,
        in_specs=(P("row", "col"),),
        out_specs=P("row", "col"),
        check_vma=False,
    )
```

time: 1590 us -> 282 us (0.18)
  waiting for transfers between devices: 1220 us -> 0 us
  Pallas kernels: 0 us -> 281 us
  other arithmetic: 232 us -> 0 us
  matrix products: 94 us -> 0 us
  local copies, waits for them, and re-layouts: 20.8 us -> 0 us
  between operations: 19.9 us -> 0.03 us
    psum x12 -> x0, waiting for transfers between devices: 1220 us -> none  [the longest x6 640 us: spread(): return lax.psum(block, axis)]
    pallas_call x0 -> x8, Pallas kernels: none -> 281 us  [the longest x2 114 us: share_image(): pl.pallas_call(image_kernel, out_shape=(tall, tall, jax.ShapeDtypeStruct(...]
    another operation x36 -> x0, other arithmetic: 218 us -> none  [the longest x27 138 us: lower_inverse(): lower_factor = jnp.linalg.cholesky(square)]
    dot_general x72 -> x0, matrix products: 88.1 us -> none  [matmul(): lax.dot_general(first_op, second_op, (((first_dim,), (second_dim,)), ((),...]
    another operation x37 -> x0, local copies, waits for them, and re-layouts: 16 us -> none  [the longest x29 15.9 us: lower_inverse(): lax.linalg.triangular_solve(lower_factor, identity, left_side=True, lower...]
  transfers between devices with their start and end apart: 12 -> 0, of which waited for: 12 -> 0; matrix products, arithmetic and copies ran while one was open for 3% -> 0% of each run, Pallas kernels for 0% -> 0%
where the time goes in v1:
time: 282 us
  Pallas kernels  281 us (100%)
    pallas_call x2, Pallas kernels, share_image(): pl.pallas_call(image_kernel, out_shape=(tall, tall, jax.ShapeDtypeStruct(...  114 us
    pallas_call x2, Pallas kernels, share_panel(): pl.pallas_call(functools.partial(panel_kernel, panel), out_shape=(tall, t...  84.5 us
    pallas_call x2, Pallas kernels, factor(): pl.pallas_call(functools.partial(factor_kernel, panel), out_shape=(tall,...  60.7 us
    pallas_call x2, Pallas kernels, update(): pl.pallas_call(update_kernel, out_shape=jax.ShapeDtypeStruct((size, size)...  22.7 us

profile of v1, /device:TPU:1, one launch (start us, length us, event | category | flops | bytes accessed | tf_op | source)
XLA Modules:
  0.0 281.5 jit_solution(1736473271089585454)
XLA Ops:
  0.0 44.0 %share_panel_0.1 = (f32[1024,256]{1,0:T(8,128)}, f32[1024,256]{1,0:T(8,128)}, f32[16,32,256]{2,1,0:T(8,128)}) custom-call(f32[1024,1024]{1,0:T(8,128)} %a_ref.5), custom_call_target="tpu_custom_call" | custom-call | tf_op jit(solution)/shard_map/share_panel_0/pallas_call | solution.py:412
  44.0 30.3 %factor_0.1 = (f32[1024,256]{1,0:T(8,128)}, f32[1024,256]{1,0:T(8,128)}, f32[256,256]{1,0:T(8,128)}, f32[1024,256]{1,0:T(8,128)}, f32[256,256]{1,0:T(8,128)}) custom-call(f32[1024,1024]{1,0:T(8,128)} %a_ref.5, f32[1024,256]{1,0:T(8,128)} %get-tuple-element.27.pr_ref, f32[1024,256]{1,0:T(8,128)} %get-tuple-element.28.pq_ref, ...), custom_call_target="tpu_custom_call" | custom-call | tf_op jit(solution)/shard_map/factor_0/pallas_call | solution.py:168
  74.3 56.5 %share_image.2 = (f32[1024,256]{1,0:T(8,128)}, f32[1024,256]{1,0:T(8,128)}, f32[256,256]{1,0:T(8,128)}) custom-call(f32[1024,256]{1,0:T(8,128)} %get-tuple-element.31.x_ref, f32[256,256]{1,0:T(8,128)} %get-tuple-element.32.kp_ref, f32[256,256]{1,0:T(8,128)} %get-tuple-element.33.mid_ref), custom_call_target="tpu_custom_call" | custom-call | tf_op jit(solution)/shard_map/share_image/pallas_call | solution.py:521
  130.8 11.3 %update.2.a_ref = f32[1024,1024]{1,0:T(8,128)} custom-call(f32[1024,1024]{1,0:T(8,128)} %a_ref.5, f32[1024,256]{1,0:T(8,128)} %get-tuple-element.30.vr_ref, f32[1024,256]{1,0:T(8,128)} %get-tuple-element.34.cp_ref, f32[1024,256]{1,0:T(8,128)} %get-tuple-element.35.vq_ref, f32[1024,256]{1,0:T(8,128)} %get-tuple-element.36.cq_ref, ...), custom_call_target="tpu_custom_call" | custom-call | tf_op jit(solution)/shard_map/update/pallas_call | solution.py:568
  142.1 40.6 %share_panel_1.1 = (f32[1024,256]{1,0:T(8,128)}, f32[1024,256]{1,0:T(8,128)}, f32[16,32,256]{2,1,0:T(8,128)}) custom-call(f32[1024,1024]{1,0:T(8,128)} %update.2.a_ref), custom_call_target="tpu_custom_call" | custom-call | tf_op jit(solution)/shard_map/share_panel_1/pallas_call | solution.py:412
  182.7 30.4 %factor_1.1 = (f32[1024,256]{1,0:T(8,128)}, f32[1024,256]{1,0:T(8,128)}, f32[256,256]{1,0:T(8,128)}, f32[1024,256]{1,0:T(8,128)}, f32[256,256]{1,0:T(8,128)}) custom-call(f32[1024,1024]{1,0:T(8,128)} %update.2.a_ref, f32[1024,256]{1,0:T(8,128)} %get-tuple-element.38.pr_ref, f32[1024,256]{1,0:T(8,128)} %get-tuple-element.39.pq_ref, ...), custom_call_target="tpu_custom_call" | custom-call | tf_op jit(solution)/shard_map/factor_1/pallas_call | solution.py:168
  213.1 57.1 %share_image.3 = (f32[1024,256]{1,0:T(8,128)}, f32[1024,256]{1,0:T(8,128)}, f32[256,256]{1,0:T(8,128)}) custom-call(f32[1024,256]{1,0:T(8,128)} %get-tuple-element.42.x_ref, f32[256,256]{1,0:T(8,128)} %get-tuple-element.43.kp_ref, f32[256,256]{1,0:T(8,128)} %get-tuple-element.44.mid_ref), custom_call_target="tpu_custom_call" | custom-call | tf_op jit(solution)/shard_map/share_image/pallas_call | solution.py:521
  270.2 11.3 %update.3 = f32[1024,1024]{1,0:T(8,128)} custom-call(f32[1024,1024]{1,0:T(8,128)} %update.2.a_ref, f32[1024,256]{1,0:T(8,128)} %get-tuple-element.41.vr_ref, f32[1024,256]{1,0:T(8,128)} %get-tuple-element.45.cp_ref, f32[1024,256]{1,0:T(8,128)} %get-tuple-element.46.vq_ref, f32[1024,256]{1,0:T(8,128)} %get-tuple-element.47.cq_ref, ...), custom_call_target="tpu_custom_call" | custom-call | tf_op jit(solution)/shard_map/update/pallas_call | solution.py:568

commit v2 on v1

v2 whole, which is shorter than its diff:
```python
import functools

import jax
import jax.numpy as jnp
from jax import lax
from jax.experimental import pallas as pl
from jax.experimental.pallas import tpu as pltpu
from jax.sharding import PartitionSpec as P

B = 256
PANELS = 2
NS_STEPS = 12
D = 16
PIECE = 64
SLICE = 16
MESH = pl.DeviceIdType.MESH
HIGHEST = lax.Precision.HIGHEST
VMEM_LIMIT = 56 * 1024 * 1024


def dot(first, second, first_dim, second_dim):
    return lax.dot_general(
        first,
        second,
        (((first_dim,), (second_dim,)), ((), ())),
        precision=HIGHEST,
        preferred_element_type=jnp.float32,
    )


def split(value):
    high = value.astype(jnp.bfloat16)
    return high, (value - high.astype(jnp.float32)).astype(jnp.bfloat16)


def dot_split(first, second, first_dim, second_dim):
    def one(x, y):
        return lax.dot_general(
            x, y, (((first_dim,), (second_dim,)), ((), ())), preferred_element_type=jnp.float32
        )

    return one(first[0], second[0]) + (one(first[0], second[1]) + one(first[1], second[0]))


def dot3(first, second, first_dim, second_dim):
    return dot_split(split(first), split(second), first_dim, second_dim)


def sublane(x, j):
    return jnp.broadcast_to(x[j : j + 1, :], x.shape)


def chol_inverse_128(d_ref):
    n = 128
    sub = lax.broadcasted_iota(jnp.int32, (8, n), 0)
    lane = lax.broadcasted_iota(jnp.int32, (8, n), 1)
    rows = [d_ref[8 * g : 8 * g + 8, :] for g in range(n // 8)]
    for g in range(n // 8):
        k0 = 8 * g
        own = (lane >= k0) & (lane < k0 + 8)
        unit = jnp.where(lane == sub + k0, 1.0, 0.0)
        cur = rows[g]
        cols = [jnp.broadcast_to(cur[:, k0 + j : k0 + j + 1], (8, n)) for j in range(8)]
        cur = jnp.where(own, unit, cur)
        recips, factors, pivots = [], {}, []
        diag = jnp.ones((8, n), jnp.float32)
        for j in range(8):
            d = sublane(cols[j], j)
            recips.append(1.0 / d)
            diag = jnp.where(sub == j, d, diag)
            f = jnp.where(sub > j, cols[j] * recips[j], 0.0)
            for l in range(j + 1, 8):
                factors[j, l] = sublane(cols[l], j)
                cols[l] = cols[l] - f * factors[j, l]
            pivots.append(sublane(cur, j))
            cur = cur - f * pivots[j]
        d_ref[k0 : k0 + 8, :] = jnp.where(lane < k0 + 8, cur, 0.0) / jnp.sqrt(diag)
        for i in range(g + 1, n // 8):
            low = rows[i]
            cols = [jnp.broadcast_to(low[:, k0 + j : k0 + j + 1], (8, n)) for j in range(8)]
            low = jnp.where(own, 0.0, low)
            for j in range(8):
                f = cols[j] * recips[j]
                for l in range(j + 1, 8):
                    cols[l] = cols[l] - f * factors[j, l]
                low = low - f * pivots[j]
            rows[i] = low


def chol_inverse(gram_ref, out_ref, d_ref, half_ref, below_ref):
    half = B // 2
    d_ref[...] = gram_ref[:half, :half]

    def step(i, carry):
        chol_inverse_128(d_ref)
        half_ref[i] = d_ref[...]

        @pl.when(i == 0)
        def _():
            below = dot(gram_ref[half:, :half], d_ref[...], 1, 1)
            below_ref[...] = below
            d_ref[...] = gram_ref[half:, half:] - dot(below, below, 1, 1)

        return carry

    lax.fori_loop(0, 2, step, 0)
    first, second = half_ref[0], half_ref[1]
    out_ref[:half, :half] = first
    out_ref[:half, half:] = jnp.zeros((half, half), jnp.float32)
    out_ref[half:, :half] = -dot(second, dot(below_ref[...], first, 1, 0), 1, 0)
    out_ref[half:, half:] = second


def eye():
    r = lax.broadcasted_iota(jnp.int32, (B, B), 0)
    c = lax.broadcasted_iota(jnp.int32, (B, B), 1)
    return jnp.where(r == c, 1.0, 0.0)


def greet(p, q):
    barrier = pltpu.get_barrier_semaphore()
    for i in range(1, D):
        pl.semaphore_signal(
            barrier, inc=1, device_id=(lax.rem(p + i, D), q), device_id_type=MESH
        )
        pl.semaphore_signal(
            barrier, inc=1, device_id=(p, lax.rem(q + i, D)), device_id_type=MESH
        )

    @pl.when(p != q)
    def _():
        pl.semaphore_signal(barrier, inc=1, device_id=(q, p), device_id_type=MESH)


def await_greetings(p, q):
    barrier = pltpu.get_barrier_semaphore()

    @pl.when(p != q)
    def _():
        pl.semaphore_wait(barrier, 2 * (D - 1) + 1)

    @pl.when(p == q)
    def _():
        pl.semaphore_wait(barrier, 2 * (D - 1))


def remote(src, dst, send, recv, target):
    return pltpu.make_async_remote_copy(
        src_ref=src, dst_ref=dst, send_sem=send, recv_sem=recv,
        device_id=target, device_id_type=MESH,
    )


def piece(index):
    return pl.ds(pl.multiple_of(index * PIECE, PIECE), PIECE)


def slab(index):
    return pl.ds(pl.multiple_of(index * SLICE, SLICE), SLICE)


def gather_col_start(ref, at, send, recv, p, q):
    for i in range(1, D):
        t = lax.rem(q + i, D)
        remote(ref.at[at(q)], ref.at[at(q)], send.at[i], recv.at[q], (p, t)).start()


def gather_col_wait(ref, at, send, recv, p, q):
    for i in range(1, D):
        t = lax.rem(q + i, D)
        remote(ref.at[at(t)], ref.at[at(t)], send.at[i], recv.at[t], (p, t)).wait_recv()


def gather_col_drain(ref, at, send, recv, p, q):
    for i in range(1, D):
        t = lax.rem(q + i, D)
        remote(ref.at[at(q)], ref.at[at(q)], send.at[i], recv.at[q], (p, t)).wait_send()


def gather_row_start(ref, send, recv, p, q):
    for i in range(0, D, 2):
        t = lax.rem(p + i, D) if i else p + 1 - 2 * lax.rem(p, 2)
        remote(ref.at[piece(p)], ref.at[piece(p)], send.at[i], recv.at[p], (t, q)).start()


def gather_row_pass(ref, send, recv, p, q):
    other = p + 1 - 2 * lax.rem(p, 2)
    for i in (2, 14, 4, 12, 6, 10, 8):
        t = lax.rem(p + i, D)
        remote(ref.at[piece(t)], ref.at[piece(t)], send.at[i], recv.at[t], (t, q)).wait_recv()
        remote(ref.at[piece(t)], ref.at[piece(t)], send.at[i + 1], recv.at[t], (other, q)).start()


def gather_row_wait(ref, send, recv, p, q):
    other = p + 1 - 2 * lax.rem(p, 2)
    for i in range(0, D, 2):
        t = lax.rem(other + i, D)
        remote(ref.at[piece(t)], ref.at[piece(t)], send.at[i], recv.at[t], (other, q)).wait_recv()


def gather_row_drain(ref, send, recv, p, q):
    other = p + 1 - 2 * lax.rem(p, 2)
    for i in range(0, D, 2):
        remote(ref.at[piece(p)], ref.at[piece(p)], send.at[i], recv.at[p], (other, q)).wait_send()
        if i:
            t = lax.rem(p + i, D)
            remote(
                ref.at[piece(t)], ref.at[piece(t)], send.at[i + 1], recv.at[t], (other, q)
            ).wait_send()


def reduce_kernel(
    panel, a_ref, vr_ref, vq_ref, cp_ref, cq_ref, k_ref, mid_ref,
    a_vm, pr_ref, pq_ref, g_ref, t_ref, tall, wide, turned, gram, part, block,
    inv_ref, d_ref, half_ref, below_ref, w_ref,
    x_ref, kp_ref, parts, kparts, ksum, kpair, khalf, kz,
    load, gram_s, gram_r, block_s, block_r, gdown_s, gdown_r, tdown_s, tdown_r,
    g_s, g_r, t_s, t_r, prs_s, prs_r, pr_s, pr_r, pqs_s, pqs_r, pq_s, pq_r,
    x_s, x_r, kp_s, kp_r, pair_s, pair_r, kz_s, kz_r, half_s, half_r, k_s, k_r,
    cp_s, cp_r, turn_s, turn_r, cq_s, cq_r,
):
    p, q = lax.axis_index("row"), lax.axis_index("col")
    row_owner, col_owner, top_col = p == panel, q == panel, q == panel + 1
    core = lax.rem(p, 2)
    other = p + 1 - 2 * core
    whole = lambda index: index
    row_peers = [lax.rem(p + i, D) for i in range(D)]
    col_peers = [lax.rem(q + i, D) for i in range(D)]

    loads = [
        pltpu.make_async_copy(a_ref.at[pl.ds(0, B)], a_vm.at[pl.ds(0, B)], load.at[0]),
        pltpu.make_async_copy(
            a_ref.at[pl.ds(B, 3 * B)], a_vm.at[pl.ds(B, 3 * B)], load.at[1]
        ),
    ]
    for copy in loads:
        copy.start()
    greet(p, q)
    loads[0].wait()

    @pl.when(row_owner)
    def _():
        wide[...] = a_vm[:B, :]

        @pl.when(q <= panel)
        def _():
            wide[:, :B] = jnp.zeros((B, B), jnp.float32)

        gram[...] = dot(wide[...], wide[...], 1, 1)

    await_greetings(p, q)

    gram_out = lambda i: remote(
        gram.at[slab(col_peers[i])], part.at[q], gram_s.at[i], gram_r.at[q], (p, col_peers[i])
    )
    block_out = lambda i: remote(
        block.at[slab(col_peers[i])], t_ref.at[col_peers[i]], block_s.at[i], block_r,
        (p, col_peers[i]),
    )
    pq_out = lambda i: remote(
        turned.at[piece(row_peers[i])], pq_ref.at[piece(row_peers[i])], pqs_s.at[i], pqs_r,
        (row_peers[i], q),
    )
    pr_out = lambda i: remote(
        tall.at[piece(col_peers[i])], pr_ref.at[piece(col_peers[i])], prs_s.at[i], prs_r,
        (p, col_peers[i]),
    )
    g_down = lambda i: remote(
        g_ref.at[q], g_ref.at[q], gdown_s.at[i], gdown_r, (row_peers[i], q)
    )
    t_down = lambda i: remote(
        t_ref.at[q], t_ref.at[q], tdown_s.at[i], tdown_r, (row_peers[i], q)
    )

    @pl.when(row_owner)
    def _():
        for i in range(1, D):
            gram_out(i).start()
        part[q] = gram[slab(q), :]

        @pl.when(top_col)
        def _():
            block[...] = wide[:, :B].T
            for i in range(1, D):
                block_out(i).start()
            t_ref[q] = block[slab(q), :]

        turned[...] = wide[...].T
        for i in range(1, D):
            pq_out(i).start()
        pq_ref[piece(p), :] = turned[piece(p), :]

    loads[1].wait()

    @pl.when(col_owner)
    def _():
        tall[...] = a_vm[:, :B]

        @pl.when(p <= panel)
        def _():
            tall[:B, :] = jnp.zeros((B, B), jnp.float32)

        for i in range(1, D):
            pr_out(i).start()
        pr_ref[piece(q), :] = tall[piece(q), :]

    @pl.when(row_owner)
    def _():
        for i in range(1, D):
            t = col_peers[i]
            remote(gram.at[slab(q)], part.at[t], gram_s.at[i], gram_r.at[t], (p, t)).wait_recv()
        total = part[0]
        for i in range(1, D):
            total = total + part[i]
        g_ref[q] = total
        for i in range(1, D):
            g_down(i).start()

        @pl.when(jnp.logical_not(top_col))
        def _():
            block_out(1).wait_recv()

        for i in range(1, D):
            t_down(i).start()

    @pl.when(jnp.logical_not(row_owner))
    def _():
        g_down(1).wait_recv()

    gather_col_start(g_ref, whole, g_s, g_r, p, q)

    @pl.when(jnp.logical_not(row_owner))
    def _():
        t_down(1).wait_recv()

    gather_col_start(t_ref, whole, t_s, t_r, p, q)

    @pl.when(jnp.logical_not(row_owner))
    def _():
        pq_out(1).wait_recv()

    gather_row_start(pq_ref, pq_s, pq_r, p, q)

    @pl.when(jnp.logical_not(col_owner))
    def _():
        pr_out(1).wait_recv()

    gather_col_start(pr_ref, piece, pr_s, pr_r, p, q)

    gather_col_wait(g_ref, whole, g_s, g_r, p, q)
    kp_ref[...] = g_ref[...].reshape(B, B)
    chol_inverse(kp_ref, inv_ref, d_ref, half_ref, below_ref)
    gather_row_pass(pq_ref, pq_s, pq_r, p, q)
    gather_col_wait(t_ref, whole, t_s, t_r, p, q)
    inverse_low = inv_ref[...]
    top = dot(t_ref[...].reshape(B, B), inverse_low, 1, 1)
    w_ref[...] = top

    def polar_step(i, carry):
        w = w_ref[...]
        s = split(w)
        w_ref[...] = 1.5 * w - 0.5 * dot_split(s, split(dot_split(s, s, 0, 0)), 1, 0)
        return carry

    lax.fori_loop(0, NS_STEPS, polar_step, 0)
    w = w_ref[...]
    cross = dot(w, top, 0, 0)
    metric = eye() + cross + cross.T + dot(w, w, 0, 0)
    guess = (40.0 / 41.0) * eye() - (8.0 / 41.0) * metric
    for i in range(4):
        mul = dot if i == 3 else dot3
        guess = guess + mul(guess, eye() - mul(metric, guess, 1, 0), 1, 0)
    mid_ref[...] = 2.0 * guess

    gather_row_wait(pq_ref, pq_s, pq_r, p, q)
    inv_split = split(inverse_low)

    def reflect(ref, out):
        def step(tile, carry):
            rows = pl.ds(pl.multiple_of(tile * B, B), B)
            out[rows, :] = dot_split(split(ref[rows, :]), inv_split, 1, 1)
            return carry

        lax.fori_loop(0, 4, step, 0)

    reflect(pq_ref, vq_ref)

    @pl.when(top_col)
    def _():
        vq_ref[:B, :] = vq_ref[:B, :] + w

    gather_col_wait(pr_ref, piece, pr_s, pr_r, p, q)
    reflect(pr_ref, vr_ref)

    @pl.when(p == panel + 1)
    def _():
        vr_ref[:B, :] = vr_ref[:B, :] + w_ref[...]

    vq = split(vq_ref[...])
    kp_ref[...] = jnp.zeros((B, B), jnp.float32)
    x_out = lambda t: remote(
        x_ref.at[piece(t)], parts.at[q], x_s.at[t], x_r.at[q], (p, t)
    )

    def product_step(number, carry):
        tile = lax.rem(q // 4 + number, 4)
        rows = pl.ds(pl.multiple_of(tile * B, B), B)
        x = dot_split(split(a_vm[rows, :]), vq, 1, 0)
        x_ref[rows, :] = x
        for i in range(4):
            t = 4 * tile + lax.rem(q + i, 4)

            @pl.when(t != q)
            def _():
                x_out(t).start()

        kp_ref[...] += dot3(vr_ref[rows, :], x, 0, 0)
        return carry

    lax.fori_loop(0, 4, product_step, 0)
    parts[q] = x_ref[piece(q), :]
    kp_out = lambda i: remote(
        kp_ref.at[slab(col_peers[i])], kparts.at[q], kp_s.at[i], kp_r.at[q], (p, col_peers[i])
    )
    for i in range(1, D):
        kp_out(i).start()
    kparts[q] = kp_ref[slab(q), :]

    for i in range(1, D):
        t = col_peers[i]
        remote(x_ref.at[piece(q)], parts.at[t], x_s.at[t], x_r.at[t], (p, t)).wait_recv()
    total = parts[0]
    for i in range(1, D):
        total = total + parts[i]
    image = dot(total, mid_ref[...], 1, 0)
    cp_ref[piece(q), :] = image
    turn_out = remote(cp_ref.at[piece(q)], cq_ref.at[piece(q)], turn_s, turn_r, (q, p))

    @pl.when(p != q)
    def _():
        turn_out.start()

    @pl.when(p == q)
    def _():
        cq_ref[piece(p), :] = image

    gather_col_start(cp_ref, piece, cp_s, cp_r, p, q)

    for i in range(1, D):
        t = col_peers[i]
        remote(kp_ref.at[slab(q)], kparts.at[t], kp_s.at[i], kp_r.at[t], (p, t)).wait_recv()
    total = kparts[0]
    for i in range(1, D):
        total = total + kparts[i]
    ksum[...] = total
    pair_out = remote(ksum, kpair, pair_s, pair_r, (other, q))
    pair_out.start()
    pair_out.wait_recv()
    khalf[...] = ksum[...] + kpair[...]
    mine = pl.ds(pl.multiple_of(core * 8, 8), 8)
    kz_out = lambda i: remote(
        khalf.at[mine], kz.at[p // 2], kz_s.at[i // 2], kz_r.at[p // 2], (row_peers[i], q)
    )
    for i in range(2, D, 2):
        kz_out(i).start()
    kz[p // 2] = khalf[mine, :]

    @pl.when(p != q)
    def _():
        remote(cp_ref.at[piece(q)], cq_ref.at[piece(p)], turn_s, turn_r, (q, p)).wait_recv()

    gather_row_start(cq_ref, cq_s, cq_r, p, q)
    for i in range(2, D, 2):
        t = row_peers[i] // 2
        remote(
            khalf.at[mine], kz.at[t], kz_s.at[i // 2], kz_r.at[t], (row_peers[i], q)
        ).wait_recv()
    total = kz[0]
    for i in range(1, D // 2):
        total = total + kz[i]
    here = pl.ds(pl.multiple_of(q * SLICE + core * 8, 8), 8)
    there = pl.ds(pl.multiple_of(q * SLICE + 8 - core * 8, 8), 8)
    k_ref[here, :] = total
    half_out = remote(k_ref.at[here], k_ref.at[here], half_s, half_r, (other, q))
    half_out.start()
    remote(k_ref.at[there], k_ref.at[there], half_s, half_r, (other, q)).wait_recv()
    gather_col_start(k_ref, slab, k_s, k_r, p, q)
    gather_row_pass(cq_ref, cq_s, cq_r, p, q)
    gather_col_wait(cp_ref, piece, cp_s, cp_r, p, q)
    gather_col_wait(k_ref, slab, k_s, k_r, p, q)
    gather_row_wait(cq_ref, cq_s, cq_r, p, q)

    gather_row_drain(cq_ref, cq_s, cq_r, p, q)
    gather_row_drain(pq_ref, pq_s, pq_r, p, q)
    for ref, at, send, recv in (
        (cp_ref, piece, cp_s, cp_r), (k_ref, slab, k_s, k_r), (pr_ref, piece, pr_s, pr_r),
        (g_ref, whole, g_s, g_r), (t_ref, whole, t_s, t_r),
    ):
        gather_col_drain(ref, at, send, recv, p, q)

    @pl.when(p != q)
    def _():
        turn_out.wait_send()

    pair_out.wait_send()
    half_out.wait_send()
    for i in range(2, D, 2):
        kz_out(i).wait_send()
    for i in range(1, D):
        kp_out(i).wait_send()
        x_out(col_peers[i]).wait_send()

    @pl.when(row_owner)
    def _():
        for i in range(1, D):
            gram_out(i).wait_send()
            pq_out(i).wait_send()
            g_down(i).wait_send()
            t_down(i).wait_send()

        @pl.when(top_col)
        def _():
            for i in range(1, D):
                block_out(i).wait_send()

    @pl.when(col_owner)
    def _():
        for i in range(1, D):
            pr_out(i).wait_send()


def reduce_panel(panel, matrix):
    vmem = pl.BlockSpec(memory_space=pltpu.VMEM)
    buffer = lambda *shape: pltpu.VMEM(shape, jnp.float32)
    tall = jax.ShapeDtypeStruct((4 * B, B), jnp.float32)
    square = jax.ShapeDtypeStruct((B, B), jnp.float32)
    many, one = pltpu.SemaphoreType.DMA((D,)), pltpu.SemaphoreType.DMA
    return pl.pallas_call(
        functools.partial(reduce_kernel, panel),
        out_shape=(tall, tall, tall, tall, square, square),
        in_specs=[pl.BlockSpec(memory_space=pl.ANY)],
        out_specs=(vmem,) * 6,
        scratch_shapes=[
            buffer(4 * B, 4 * B), buffer(4 * B, B), buffer(4 * B, B),
            buffer(D, SLICE, B), buffer(D, SLICE, B),
            buffer(4 * B, B), buffer(B, 4 * B), buffer(4 * B, B),
            buffer(B, B), buffer(D, SLICE, B), buffer(B, B),
            buffer(B, B), buffer(B // 2, B // 2), buffer(2, B // 2, B // 2),
            buffer(B // 2, B // 2), buffer(B, B),
            buffer(4 * B, B), buffer(B, B), buffer(D, PIECE, B), buffer(D, SLICE, B),
            buffer(SLICE, B), buffer(SLICE, B), buffer(SLICE, B), buffer(D // 2, 8, B),
            pltpu.SemaphoreType.DMA((2,)),
            many, many, many, one, many, one, many, one,
            many, many, many, many, many, one, many, many, many, one, many, many,
            many, many, many, many, one, one, many, many, one, one, many, many,
            many, many, one, one, many, many,
        ],
        compiler_params=pltpu.CompilerParams(
            collective_id=1 + panel, has_side_effects=True, vmem_limit_bytes=VMEM_LIMIT
        ),
        name=f"reduce_panel_{panel}",
    )(matrix)


def update_kernel(
    a_ref, vr_ref, cp_ref, vq_ref, cq_ref, k_ref, mid_ref, out_ref, right_high, right_low
):
    @pl.when(pl.program_id(0) == 0)
    def _():
        middle = mid_ref[...]
        shift = dot3(dot3(middle, k_ref[...], 1, 0), middle, 1, 0)
        shift = split(0.5 * (shift + shift.T))
        for tile in range(4):
            rows = slice(tile * B, tile * B + B)
            vq = vq_ref[rows, :]
            high, low = split(vq.T)
            right_high[:B, rows] = high
            right_low[:B, rows] = low
            other = cq_ref[rows, :] - dot_split(split(vq), shift, 1, 0)
            high, low = split(other.T)
            right_high[B:, rows] = high
            right_low[B:, rows] = low

    left = split(jnp.concatenate((cp_ref[...], vr_ref[...]), 1))
    out_ref[...] = a_ref[...] - dot_split(left, (right_high[...], right_low[...]), 1, 0)


def update(matrix, vr, cp, vq, cq, k, middle):
    rows = 128
    size = 4 * B
    whole = lambda shape: pl.BlockSpec(shape, lambda i: (0, 0))
    tile = lambda width: pl.BlockSpec((rows, width), lambda i: (i, 0))
    return pl.pallas_call(
        update_kernel,
        out_shape=jax.ShapeDtypeStruct((size, size), jnp.float32),
        grid=(size // rows,),
        in_specs=[
            tile(size), tile(B), tile(B), whole((size, B)), whole((size, B)),
            whole((B, B)), whole((B, B)),
        ],
        out_specs=tile(size),
        scratch_shapes=[pltpu.VMEM((2 * B, size), jnp.bfloat16)] * 2,
        compiler_params=pltpu.CompilerParams(vmem_limit_bytes=VMEM_LIMIT),
        name="update",
    )(matrix, vr, cp, vq, cq, k, middle)


def body(affinity):
    matrix = affinity
    for panel in range(PANELS):
        vr, vq, cp, cq, k, middle = reduce_panel(panel, matrix)
        matrix = update(matrix, vr, cp, vq, cq, k, middle)
    return matrix


def solution(mesh):
    return jax.shard_map(
        body,
        mesh=mesh,
        in_specs=(P("row", "col"),),
        out_specs=P("row", "col"),
        check_vma=False,
    )
```

time: 282 us -> 228 us (0.81)
  Pallas kernels: 281 us -> 228 us
    pallas_call x6 -> x2, Pallas kernels: 259 us -> 205 us  [reduce_panel(): pl.pallas_call(functools.partial(reduce_kernel, panel), out_shape=(tall,...]
where the time goes in v2:
time: 228 us
  Pallas kernels  228 us (100%)
    pallas_call x2, Pallas kernels, reduce_panel(): pl.pallas_call(functools.partial(reduce_kernel, panel), out_shape=(tall,...  205 us
    pallas_call x2, Pallas kernels, update(): pl.pallas_call(update_kernel, out_shape=jax.ShapeDtypeStruct((size, size)...  22.7 us

profile of v2, /device:TPU:1, one launch (start us, length us, event | category | flops | bytes accessed | tf_op | source)
XLA Modules:
  0.0 227.7 jit_solution(12624319483342302943)
XLA Ops:
  0.0 107.4 %reduce_panel_0.1 = (f32[1024,256]{1,0:T(8,128)}, f32[1024,256]{1,0:T(8,128)}, f32[1024,256]{1,0:T(8,128)}, f32[1024,256]{1,0:T(8,128)}, f32[256,256]{1,0:T(8,128)}, /*index=5*/f32[256,256]{1,0:T(8,128)}) custom-call(f32[1024,1024]{1,0:T(8,128)} %a_ref.3), custom_call_target="tpu_custom_call" | custom-call | tf_op jit(solution)/shard_map/reduce_panel_0/pallas_call | solution.py:538
  107.4 11.3 %update.2.a_ref = f32[1024,1024]{1,0:T(8,128)} custom-call(f32[1024,1024]{1,0:T(8,128)} %a_ref.3, f32[1024,256]{1,0:T(8,128)} %get-tuple-element.17.vr_ref, f32[1024,256]{1,0:T(8,128)} %get-tuple-element.18.cp_ref, f32[1024,256]{1,0:T(8,128)} %get-tuple-element.19.vq_ref, f32[1024,256]{1,0:T(8,128)} %get-tuple-element.20.cq_ref, ...), custom_call_target="tpu_custom_call" | custom-call | tf_op jit(solution)/shard_map/update/pallas_call | solution.py:593
  118.8 97.6 %reduce_panel_1.1 = (f32[1024,256]{1,0:T(8,128)}, f32[1024,256]{1,0:T(8,128)}, f32[1024,256]{1,0:T(8,128)}, f32[1024,256]{1,0:T(8,128)}, f32[256,256]{1,0:T(8,128)}, /*index=5*/f32[256,256]{1,0:T(8,128)}) custom-call(f32[1024,1024]{1,0:T(8,128)} %update.2.a_ref), custom_call_target="tpu_custom_call" | custom-call | tf_op jit(solution)/shard_map/reduce_panel_1/pallas_call | solution.py:538
  216.4 11.3 %update.3 = f32[1024,1024]{1,0:T(8,128)} custom-call(f32[1024,1024]{1,0:T(8,128)} %update.2.a_ref, f32[1024,256]{1,0:T(8,128)} %get-tuple-element.23.vr_ref, f32[1024,256]{1,0:T(8,128)} %get-tuple-element.24.cp_ref, f32[1024,256]{1,0:T(8,128)} %get-tuple-element.25.vq_ref, f32[1024,256]{1,0:T(8,128)} %get-tuple-element.26.cq_ref, ...), custom_call_target="tpu_custom_call" | custom-call | tf_op jit(solution)/shard_map/update/pallas_call | solution.py:593

commit v3 on v2

--- a/solution.py
+++ b/solution.py
@@ -1,4 +1,4 @@
-import functools
+import types
 
 import jax
 import jax.numpy as jnp
@@ -183,9 +183,10 @@
         remote(ref.at[piece(p)], ref.at[piece(p)], send.at[i], recv.at[p], (t, q)).start()
 
 
-def gather_row_pass(ref, send, recv, p, q):
+def gather_row_pass(ref, send, recv, p, q, number=None):
     other = p + 1 - 2 * lax.rem(p, 2)
-    for i in (2, 14, 4, 12, 6, 10, 8):
+    order = ((2, 14), (4, 12), (6, 10), (8,))
+    for i in sum(order, ()) if number is None else order[number]:
         t = lax.rem(p + i, D)
         remote(ref.at[piece(t)], ref.at[piece(t)], send.at[i], recv.at[t], (t, q)).wait_recv()
         remote(ref.at[piece(t)], ref.at[piece(t)], send.at[i + 1], recv.at[t], (other, q)).start()
@@ -209,16 +210,83 @@
             ).wait_send()
 
 
-def reduce_kernel(
-    panel, a_ref, vr_ref, vq_ref, cp_ref, cq_ref, k_ref, mid_ref,
-    a_vm, pr_ref, pq_ref, g_ref, t_ref, tall, wide, turned, gram, part, block,
-    inv_ref, d_ref, half_ref, below_ref, w_ref,
-    x_ref, kp_ref, parts, kparts, ksum, kpair, khalf, kz,
-    load, gram_s, gram_r, block_s, block_r, gdown_s, gdown_r, tdown_s, tdown_r,
-    g_s, g_r, t_s, t_r, prs_s, prs_r, pr_s, pr_r, pqs_s, pqs_r, pq_s, pq_r,
-    x_s, x_r, kp_s, kp_r, pair_s, pair_r, kz_s, kz_r, half_s, half_r, k_s, k_r,
-    cp_s, cp_r, turn_s, turn_r, cq_s, cq_r,
-):
+TALL, SQUARE, SLABS = (4 * B, B), (B, B), (D, SLICE, B)
+PANEL_BUFFERS = dict(
+    pr_ref=TALL, pq_ref=TALL, g_ref=SLABS, t_ref=SLABS, tall=TALL, wide=(B, 4 * B), turned=TALL,
+    gram=SQUARE, part=SLABS, block=SQUARE, x_ref=TALL, kp_ref=SQUARE, parts=(D, PIECE, B),
+    kparts=SLABS, ksum=(SLICE, B), kpair=(SLICE, B), khalf=(SLICE, B), kz=(D // 2, 8, B),
+    cp_ref=TALL, cq_ref=TALL, k_ref=SQUARE,
+)
+PANEL_MANY = (
+    "gram_s", "gram_r", "block_s", "gdown_s", "tdown_s", "g_s", "g_r", "t_s", "t_r", "prs_s",
+    "pr_s", "pr_r", "pqs_s", "pq_s", "pq_r", "x_s", "x_r", "kp_s", "kp_r", "kz_s", "kz_r",
+    "k_s", "k_r", "cp_s", "cp_r", "cq_s", "cq_r",
+)
+PANEL_ONE = (
+    "block_r", "gdown_r", "tdown_r", "prs_r", "pqs_r", "pair_s", "pair_r", "half_s", "half_r",
+    "turn_s", "turn_r",
+)
+LOCAL_BUFFERS = dict(
+    a_vm=(4 * B, 4 * B), vq_ref=TALL, mid_ref=SQUARE, inv_ref=SQUARE, d_ref=(B // 2, B // 2),
+    half_ref=(2, B // 2, B // 2), below_ref=(B // 2, B // 2), w_ref=SQUARE,
+)
+
+
+def tile_rows(tile):
+    return pl.ds(pl.multiple_of(tile * B, B), B)
+
+
+def reduce_kernel(a_ref, a_out, vr_ref, last_high, last_low, *scratch):
+    scratch = list(scratch)
+    take = lambda names: {name: scratch.pop(0) for name in names}
+    local = types.SimpleNamespace(a_ref=a_ref, a_out=a_out, vr_ref=vr_ref, **take(LOCAL_BUFFERS))
+    local.last = (last_high, last_low)
+    local.turned_vq = (scratch.pop(0), scratch.pop(0))
+    local.load, local.store = scratch.pop(0), scratch.pop(0)
+    sets = [
+        types.SimpleNamespace(**take(PANEL_BUFFERS), **take(PANEL_MANY), **take(PANEL_ONE))
+        for _ in range(PANELS)
+    ]
+    local.loads = [
+        pltpu.make_async_copy(
+            a_ref.at[pl.ds(0, B)], local.a_vm.at[pl.ds(0, B)], local.load.at[0]
+        ),
+        pltpu.make_async_copy(
+            a_ref.at[pl.ds(B, 3 * B)], local.a_vm.at[pl.ds(B, 3 * B)], local.load.at[1]
+        ),
+    ]
+    for copy in local.loads:
+        copy.start()
+    greet(lax.axis_index("row"), lax.axis_index("col"))
+    local.loads[0].wait()
+    drains = [one_panel(panel, local, sets[panel]) for panel in range(PANELS)]
+    for drain in drains:
+        drain()
+    pltpu.make_async_copy(local.a_vm, a_out, local.store).wait()
+
+
+def subtract(a_vm, left, right, rows):
+    a_vm[rows, :] -= dot_split(split(left[rows, :]), (right[0][...], right[1][...]), 1, 0)
+
+
+def one_panel(panel, local, refs):
+    a_vm, vr_ref, vq_ref, mid_ref = local.a_vm, local.vr_ref, local.vq_ref, local.mid_ref
+    inv_ref, w_ref = local.inv_ref, local.w_ref
+    pr_ref, pq_ref, g_ref, t_ref = refs.pr_ref, refs.pq_ref, refs.g_ref, refs.t_ref
+    tall, wide, turned, gram = refs.tall, refs.wide, refs.turned, refs.gram
+    part, block, x_ref, kp_ref = refs.part, refs.block, refs.x_ref, refs.kp_ref
+    parts, kparts, ksum, kpair = refs.parts, refs.kparts, refs.ksum, refs.kpair
+    khalf, kz, cp_ref, cq_ref = refs.khalf, refs.kz, refs.cp_ref, refs.cq_ref
+    k_ref, gram_s, gram_r, block_s = refs.k_ref, refs.gram_s, refs.gram_r, refs.block_s
+    gdown_s, tdown_s, g_s, g_r = refs.gdown_s, refs.tdown_s, refs.g_s, refs.g_r
+    t_s, t_r, prs_s, pr_s = refs.t_s, refs.t_r, refs.prs_s, refs.pr_s
+    pr_r, pqs_s, pq_s, pq_r = refs.pr_r, refs.pqs_s, refs.pq_s, refs.pq_r
+    x_s, x_r, kp_s, kp_r = refs.x_s, refs.x_r, refs.kp_s, refs.kp_r
+    kz_s, kz_r, k_s, k_r = refs.kz_s, refs.kz_r, refs.k_s, refs.k_r
+    cp_s, cp_r, cq_s, cq_r = refs.cp_s, refs.cp_r, refs.cq_s, refs.cq_r
+    block_r, gdown_r, tdown_r, prs_r = refs.block_r, refs.gdown_r, refs.tdown_r, refs.prs_r
+    pqs_r, pair_s, pair_r, half_s = refs.pqs_r, refs.pair_s, refs.pair_r, refs.half_s
+    half_r, turn_s, turn_r = refs.half_r, refs.turn_s, refs.turn_r
     p, q = lax.axis_index("row"), lax.axis_index("col")
     row_owner, col_owner, top_col = p == panel, q == panel, q == panel + 1
     core = lax.rem(p, 2)
@@ -227,17 +295,6 @@
     row_peers = [lax.rem(p + i, D) for i in range(D)]
     col_peers = [lax.rem(q + i, D) for i in range(D)]
 
-    loads = [
-        pltpu.make_async_copy(a_ref.at[pl.ds(0, B)], a_vm.at[pl.ds(0, B)], load.at[0]),
-        pltpu.make_async_copy(
-            a_ref.at[pl.ds(B, 3 * B)], a_vm.at[pl.ds(B, 3 * B)], load.at[1]
-        ),
-    ]
-    for copy in loads:
-        copy.start()
-    greet(p, q)
-    loads[0].wait()
-
     @pl.when(row_owner)
     def _():
         wide[...] = a_vm[:B, :]
@@ -248,7 +305,8 @@
 
         gram[...] = dot(wide[...], wide[...], 1, 1)
 
-    await_greetings(p, q)
+    if panel == 0:
+        await_greetings(p, q)
 
     gram_out = lambda i: remote(
         gram.at[slab(col_peers[i])], part.at[q], gram_s.at[i], gram_r.at[q], (p, col_peers[i])
@@ -290,7 +348,11 @@
             pq_out(i).start()
         pq_ref[piece(p), :] = turned[piece(p), :]
 
-    loads[1].wait()
+    if panel == 0:
+        local.loads[1].wait()
+    else:
+        for tile in range(1, 4):
+            subtract(a_vm, vr_ref, local.last, slice(tile * B, tile * B + B))
 
     @pl.when(col_owner)
     def _():
@@ -349,7 +411,7 @@
 
     gather_col_wait(g_ref, whole, g_s, g_r, p, q)
     kp_ref[...] = g_ref[...].reshape(B, B)
-    chol_inverse(kp_ref, inv_ref, d_ref, half_ref, below_ref)
+    chol_inverse(kp_ref, inv_ref, local.d_ref, local.half_ref, local.below_ref)
     gather_row_pass(pq_ref, pq_s, pq_r, p, q)
     gather_col_wait(t_ref, whole, t_s, t_r, p, q)
     inverse_low = inv_ref[...]
@@ -359,7 +421,7 @@
     def polar_step(i, carry):
         w = w_ref[...]
         s = split(w)
-        w_ref[...] = 1.5 * w - 0.5 * dot_split(s, split(dot_split(s, s, 0, 0)), 1, 0)
+        w_ref[...] = 1.5 * w - 0.5 * dot_split(split(dot_split(s, s, 1, 1)), s, 1, 0)
         return carry
 
     lax.fori_loop(0, NS_STEPS, polar_step, 0)
@@ -425,6 +487,10 @@
     for i in range(1, D):
         kp_out(i).start()
     kparts[q] = kp_ref[slab(q), :]
+
+    for tile in range(4):
+        rows = slice(tile * B, tile * B + B)
+        local.turned_vq[0][:, rows], local.turned_vq[1][:, rows] = split(vq_ref[rows, :].T)
 
     for i in range(1, D):
         t = col_peers[i]
@@ -485,132 +551,123 @@
     half_out.start()
     remote(k_ref.at[there], k_ref.at[there], half_s, half_r, (other, q)).wait_recv()
     gather_col_start(k_ref, slab, k_s, k_r, p, q)
-    gather_row_pass(cq_ref, cq_s, cq_r, p, q)
-    gather_col_wait(cp_ref, piece, cp_s, cp_r, p, q)
+    for number in range(4):
+        tile = lax.rem(q // 4 + number, 4)
+        for i in range(4):
+            t = 4 * tile + lax.rem(q + i, 4)
+
+            @pl.when(t != q)
+            def _():
+                remote(
+                    cp_ref.at[piece(t)], cp_ref.at[piece(t)], cp_s.at[0], cp_r.at[t], (p, t)
+                ).wait_recv()
+
+        subtract(a_vm, cp_ref, local.turned_vq, tile_rows(tile))
+        gather_row_pass(cq_ref, cq_s, cq_r, p, q, number)
+    if panel == PANELS - 1:
+        pltpu.make_async_copy(a_vm, local.a_out, local.store).start()
     gather_col_wait(k_ref, slab, k_s, k_r, p, q)
+    middle = mid_ref[...]
+    shift = dot3(dot3(middle, k_ref[...], 1, 0), middle, 1, 0)
+    shift = split(0.5 * (shift + shift.T))
     gather_row_wait(cq_ref, cq_s, cq_r, p, q)
-
-    gather_row_drain(cq_ref, cq_s, cq_r, p, q)
-    gather_row_drain(pq_ref, pq_s, pq_r, p, q)
-    for ref, at, send, recv in (
-        (cp_ref, piece, cp_s, cp_r), (k_ref, slab, k_s, k_r), (pr_ref, piece, pr_s, pr_r),
-        (g_ref, whole, g_s, g_r), (t_ref, whole, t_s, t_r),
-    ):
-        gather_col_drain(ref, at, send, recv, p, q)
-
-    @pl.when(p != q)
-    def _():
-        turn_out.wait_send()
-
-    pair_out.wait_send()
-    half_out.wait_send()
-    for i in range(2, D, 2):
-        kz_out(i).wait_send()
-    for i in range(1, D):
-        kp_out(i).wait_send()
-        x_out(col_peers[i]).wait_send()
-
-    @pl.when(row_owner)
-    def _():
-        for i in range(1, D):
-            gram_out(i).wait_send()
-            pq_out(i).wait_send()
-            g_down(i).wait_send()
-            t_down(i).wait_send()
-
-        @pl.when(top_col)
+    for tile in range(4):
+        rows = slice(tile * B, tile * B + B)
+        rest = cq_ref[rows, :] - dot_split(split(vq_ref[rows, :]), shift, 1, 0)
+        local.last[0][:, rows], local.last[1][:, rows] = split(rest.T)
+    if panel < PANELS - 1:
+        subtract(a_vm, vr_ref, local.last, slice(0, B))
+
+    def drain():
+        gather_row_drain(cq_ref, cq_s, cq_r, p, q)
+        gather_row_drain(pq_ref, pq_s, pq_r, p, q)
+        for ref, at, send, recv in (
+            (cp_ref, piece, cp_s, cp_r), (k_ref, slab, k_s, k_r), (pr_ref, piece, pr_s, pr_r),
+            (g_ref, whole, g_s, g_r), (t_ref, whole, t_s, t_r),
+        ):
+            gather_col_drain(ref, at, send, recv, p, q)
+
+        @pl.when(p != q)
+        def _():
+            turn_out.wait_send()
+
+        pair_out.wait_send()
+        half_out.wait_send()
+        for i in range(2, D, 2):
+            kz_out(i).wait_send()
+        for i in range(1, D):
+            kp_out(i).wait_send()
+            x_out(col_peers[i]).wait_send()
+
+        @pl.when(row_owner)
         def _():
             for i in range(1, D):
-                block_out(i).wait_send()
-
-    @pl.when(col_owner)
-    def _():
-        for i in range(1, D):
-            pr_out(i).wait_send()
-
-
-def reduce_panel(panel, matrix):
-    vmem = pl.BlockSpec(memory_space=pltpu.VMEM)
-    buffer = lambda *shape: pltpu.VMEM(shape, jnp.float32)
-    tall = jax.ShapeDtypeStruct((4 * B, B), jnp.float32)
-    square = jax.ShapeDtypeStruct((B, B), jnp.float32)
+                gram_out(i).wait_send()
+                pq_out(i).wait_send()
+                g_down(i).wait_send()
+                t_down(i).wait_send()
+
+            @pl.when(top_col)
+            def _():
+                for i in range(1, D):
+                    block_out(i).wait_send()
+
+        @pl.when(col_owner)
+        def _():
+            for i in range(1, D):
+                pr_out(i).wait_send()
+
+    return drain
+
+
+def reduce_panels(matrix):
+    vmem, anywhere = pl.BlockSpec(memory_space=pltpu.VMEM), pl.BlockSpec(memory_space=pl.ANY)
+    buffers = lambda shapes: [pltpu.VMEM(shape, jnp.float32) for shape in shapes.values()]
     many, one = pltpu.SemaphoreType.DMA((D,)), pltpu.SemaphoreType.DMA
+    right = jax.ShapeDtypeStruct((B, 4 * B), jnp.bfloat16)
+    panel_set = buffers(PANEL_BUFFERS) + [many] * len(PANEL_MANY) + [one] * len(PANEL_ONE)
     return pl.pallas_call(
-        functools.partial(reduce_kernel, panel),
-        out_shape=(tall, tall, tall, tall, square, square),
-        in_specs=[pl.BlockSpec(memory_space=pl.ANY)],
-        out_specs=(vmem,) * 6,
-        scratch_shapes=[
-            buffer(4 * B, 4 * B), buffer(4 * B, B), buffer(4 * B, B),
-            buffer(D, SLICE, B), buffer(D, SLICE, B),
-            buffer(4 * B, B), buffer(B, 4 * B), buffer(4 * B, B),
-            buffer(B, B), buffer(D, SLICE, B), buffer(B, B),
-            buffer(B, B), buffer(B // 2, B // 2), buffer(2, B // 2, B // 2),
-            buffer(B // 2, B // 2), buffer(B, B),
-            buffer(4 * B, B), buffer(B, B), buffer(D, PIECE, B), buffer(D, SLICE, B),
-            buffer(SLICE, B), buffer(SLICE, B), buffer(SLICE, B), buffer(D // 2, 8, B),
-            pltpu.SemaphoreType.DMA((2,)),
-            many, many, many, one, many, one, many, one,
-            many, many, many, many, many, one, many, many, many, one, many, many,
-            many, many, many, many, one, one, many, many, one, one, many, many,
-            many, many, one, one, many, many,
-        ],
+        reduce_kernel,
+        out_shape=(
+            jax.ShapeDtypeStruct((4 * B, 4 * B), jnp.float32),
+            jax.ShapeDtypeStruct(TALL, jnp.float32), right, right,
+        ),
+        in_specs=[anywhere],
+        out_specs=(anywhere, vmem, vmem, vmem),
+        scratch_shapes=buffers(LOCAL_BUFFERS)
+        + [pltpu.VMEM((B, 4 * B), jnp.bfloat16)] * 2
+        + [pltpu.SemaphoreType.DMA((2,)), one]
+        + panel_set * PANELS,
         compiler_params=pltpu.CompilerParams(
-            collective_id=1 + panel, has_side_effects=True, vmem_limit_bytes=VMEM_LIMIT
+            collective_id=1, has_side_effects=True, vmem_limit_bytes=VMEM_LIMIT
         ),
-        name=f"reduce_panel_{panel}",
+        name="reduce_panels",
     )(matrix)
 
 
-def update_kernel(
-    a_ref, vr_ref, cp_ref, vq_ref, cq_ref, k_ref, mid_ref, out_ref, right_high, right_low
-):
-    @pl.when(pl.program_id(0) == 0)
-    def _():
-        middle = mid_ref[...]
-        shift = dot3(dot3(middle, k_ref[...], 1, 0), middle, 1, 0)
-        shift = split(0.5 * (shift + shift.T))
-        for tile in range(4):
-            rows = slice(tile * B, tile * B + B)
-            vq = vq_ref[rows, :]
-            high, low = split(vq.T)
-            right_high[:B, rows] = high
-            right_low[:B, rows] = low
-            other = cq_ref[rows, :] - dot_split(split(vq), shift, 1, 0)
-            high, low = split(other.T)
-            right_high[B:, rows] = high
-            right_low[B:, rows] = low
-
-    left = split(jnp.concatenate((cp_ref[...], vr_ref[...]), 1))
-    out_ref[...] = a_ref[...] - dot_split(left, (right_high[...], right_low[...]), 1, 0)
-
-
-def update(matrix, vr, cp, vq, cq, k, middle):
-    rows = 128
-    size = 4 * B
-    whole = lambda shape: pl.BlockSpec(shape, lambda i: (0, 0))
+def finish_kernel(a_ref, vr_ref, high_ref, low_ref, out_ref):
+    out_ref[...] = a_ref[...] - dot_split(
+        split(vr_ref[...]), (high_ref[...], low_ref[...]), 1, 0
+    )
+
+
+def finish(matrix, vr, high, low):
+    rows, size = 128, 4 * B
     tile = lambda width: pl.BlockSpec((rows, width), lambda i: (i, 0))
+    whole = pl.BlockSpec((B, size), lambda i: (0, 0))
     return pl.pallas_call(
-        update_kernel,
+        finish_kernel,
         out_shape=jax.ShapeDtypeStruct((size, size), jnp.float32),
         grid=(size // rows,),
-        in_specs=[
-            tile(size), tile(B), tile(B), whole((size, B)), whole((size, B)),
-            whole((B, B)), whole((B, B)),
-        ],
+        in_specs=[tile(size), tile(B), whole, whole],
         out_specs=tile(size),
-        scratch_shapes=[pltpu.VMEM((2 * B, size), jnp.bfloat16)] * 2,
         compiler_params=pltpu.CompilerParams(vmem_limit_bytes=VMEM_LIMIT),
-        name="update",
-    )(matrix, vr, cp, vq, cq, k, middle)
+        name="finish",
+    )(matrix, vr, high, low)
 
 
 def body(affinity):
-    matrix = affinity
-    for panel in range(PANELS):
-        vr, vq, cp, cq, k, middle = reduce_panel(panel, matrix)
-        matrix = update(matrix, vr, cp, vq, cq, k, middle)
-    return matrix
+    return finish(*reduce_panels(affinity))
 
 
 def solution(mesh):

time: 228 us -> 210 us (0.921)
  Pallas kernels: 228 us -> 207 us
    pallas_call x4 -> x2, Pallas kernels: 228 us -> 207 us  [the longest x1 199 us: reduce_panels(): pl.pallas_call(reduce_kernel, out_shape=(jax.ShapeDtypeStruct((4 * B, 4 *...]
where the time goes in v3:
time: 210 us; the launch traced here: 207 us
  Pallas kernels  207 us (99%)
    pallas_call x1, Pallas kernels, reduce_panels(): pl.pallas_call(reduce_kernel, out_shape=(jax.ShapeDtypeStruct((4 * B, 4 *...  199 us
    pallas_call x1, Pallas kernels, finish(): pl.pallas_call(finish_kernel, out_shape=jax.ShapeDtypeStruct((size, size)...  8.26 us

profile of v3, /device:TPU:1, one launch (start us, length us, event | category | flops | bytes accessed | tf_op | source)
XLA Modules:
  0.0 207.4 jit_solution(6439084926687257931)
XLA Ops:
  0.0 199.2 %reduce_panels.1 = (f32[1024,1024]{1,0:T(8,128)}, f32[1024,256]{1,0:T(8,128)}, bf16[256,1024]{1,0:T(8,128)(2,1)}, bf16[256,1024]{1,0:T(8,128)(2,1)}) custom-call(f32[1024,1024]{1,0:T(8,128)} %a_ref.1), custom_call_target="tpu_custom_call" | custom-call | tf_op jit(solution)/shard_map/reduce_panels/pallas_call | solution.py:629
  199.2 8.3 %finish.1 = f32[1024,1024]{1,0:T(8,128)} custom-call(f32[1024,1024]{1,0:T(8,128)} %get-tuple-element.9.a_ref, f32[1024,256]{1,0:T(8,128)} %get-tuple-element.10.vr_ref, bf16[256,1024]{1,0:T(8,128)(2,1)} %get-tuple-element.11.high_ref, bf16[256,1024]{1,0:T(8,128)(2,1)} %get-tuple-element.12.low_ref), custom_call_target="tpu_custom_call" | custom-call | tf_op jit(solution)/shard_map/finish/pallas_call | solution.py:658

commit v4 on v3

--- a/solution.py
+++ b/solution.py
@@ -68,12 +68,12 @@
             d = sublane(cols[j], j)
             recips.append(1.0 / d)
             diag = jnp.where(sub == j, d, diag)
-            f = jnp.where(sub > j, cols[j] * recips[j], 0.0)
+            f = cols[j] * recips[j]
             for l in range(j + 1, 8):
                 factors[j, l] = sublane(cols[l], j)
                 cols[l] = cols[l] - f * factors[j, l]
             pivots.append(sublane(cur, j))
-            cur = cur - f * pivots[j]
+            cur = cur - jnp.where(sub > j, f, 0.0) * pivots[j]
         d_ref[k0 : k0 + 8, :] = jnp.where(lane < k0 + 8, cur, 0.0) / jnp.sqrt(diag)
         for i in range(g + 1, n // 8):
             low = rows[i]
@@ -155,6 +155,14 @@
     return pl.ds(pl.multiple_of(index * PIECE, PIECE), PIECE)
 
 
+def half_piece(half):
+    size = PIECE // 2
+    return lambda index: pl.ds(pl.multiple_of(index * PIECE + half * size, size), size)
+
+
+HALVES = (half_piece(0), half_piece(1))
+
+
 def slab(index):
     return pl.ds(pl.multiple_of(index * SLICE, SLICE), SLICE)
 
@@ -177,36 +185,40 @@
         remote(ref.at[at(q)], ref.at[at(q)], send.at[i], recv.at[q], (p, t)).wait_send()
 
 
-def gather_row_start(ref, send, recv, p, q):
+def gather_row_start(ref, send, recv, p, q, at=None):
+    at = at or piece
     for i in range(0, D, 2):
         t = lax.rem(p + i, D) if i else p + 1 - 2 * lax.rem(p, 2)
-        remote(ref.at[piece(p)], ref.at[piece(p)], send.at[i], recv.at[p], (t, q)).start()
-
-
-def gather_row_pass(ref, send, recv, p, q, number=None):
+        remote(ref.at[at(p)], ref.at[at(p)], send.at[i], recv.at[p], (t, q)).start()
+
+
+def gather_row_pass(ref, send, recv, p, q, number=None, at=None):
     other = p + 1 - 2 * lax.rem(p, 2)
     order = ((2, 14), (4, 12), (6, 10), (8,))
+    at = at or piece
     for i in sum(order, ()) if number is None else order[number]:
         t = lax.rem(p + i, D)
-        remote(ref.at[piece(t)], ref.at[piece(t)], send.at[i], recv.at[t], (t, q)).wait_recv()
-        remote(ref.at[piece(t)], ref.at[piece(t)], send.at[i + 1], recv.at[t], (other, q)).start()
-
-
-def gather_row_wait(ref, send, recv, p, q):
+        remote(ref.at[at(t)], ref.at[at(t)], send.at[i], recv.at[t], (t, q)).wait_recv()
+        remote(ref.at[at(t)], ref.at[at(t)], send.at[i + 1], recv.at[t], (other, q)).start()
+
+
+def gather_row_wait(ref, send, recv, p, q, at=None):
     other = p + 1 - 2 * lax.rem(p, 2)
+    at = at or piece
     for i in range(0, D, 2):
         t = lax.rem(other + i, D)
-        remote(ref.at[piece(t)], ref.at[piece(t)], send.at[i], recv.at[t], (other, q)).wait_recv()
-
-
-def gather_row_drain(ref, send, recv, p, q):
+        remote(ref.at[at(t)], ref.at[at(t)], send.at[i], recv.at[t], (other, q)).wait_recv()
+
+
+def gather_row_drain(ref, send, recv, p, q, at=None):
     other = p + 1 - 2 * lax.rem(p, 2)
+    at = at or piece
     for i in range(0, D, 2):
-        remote(ref.at[piece(p)], ref.at[piece(p)], send.at[i], recv.at[p], (other, q)).wait_send()
+        remote(ref.at[at(p)], ref.at[at(p)], send.at[i], recv.at[p], (other, q)).wait_send()
         if i:
             t = lax.rem(p + i, D)
             remote(
-                ref.at[piece(t)], ref.at[piece(t)], send.at[i + 1], recv.at[t], (other, q)
+                ref.at[at(t)], ref.at[at(t)], send.at[i + 1], recv.at[t], (other, q)
             ).wait_send()
 
 
@@ -221,10 +233,11 @@
     "gram_s", "gram_r", "block_s", "gdown_s", "tdown_s", "g_s", "g_r", "t_s", "t_r", "prs_s",
     "pr_s", "pr_r", "pqs_s", "pq_s", "pq_r", "x_s", "x_r", "kp_s", "kp_r", "kz_s", "kz_r",
     "k_s", "k_r", "cp_s", "cp_r", "cq_s", "cq_r",
+    "x2_s", "x2_r", "cp2_s", "cp2_r", "cq2_s", "cq2_r",
 )
 PANEL_ONE = (
     "block_r", "gdown_r", "tdown_r", "prs_r", "pqs_r", "pair_s", "pair_r", "half_s", "half_r",
-    "turn_s", "turn_r",
+    "turn_s", "turn_r", "turn2_s", "turn2_r",
 )
 LOCAL_BUFFERS = dict(
     a_vm=(4 * B, 4 * B), vq_ref=TALL, mid_ref=SQUARE, inv_ref=SQUARE, d_ref=(B // 2, B // 2),
@@ -281,12 +294,15 @@
     gdown_s, tdown_s, g_s, g_r = refs.gdown_s, refs.tdown_s, refs.g_s, refs.g_r
     t_s, t_r, prs_s, pr_s = refs.t_s, refs.t_r, refs.prs_s, refs.pr_s
     pr_r, pqs_s, pq_s, pq_r = refs.pr_r, refs.pqs_s, refs.pq_s, refs.pq_r
-    x_s, x_r, kp_s, kp_r = refs.x_s, refs.x_r, refs.kp_s, refs.kp_r
+    kp_s, kp_r = refs.kp_s, refs.kp_r
     kz_s, kz_r, k_s, k_r = refs.kz_s, refs.kz_r, refs.k_s, refs.k_r
-    cp_s, cp_r, cq_s, cq_r = refs.cp_s, refs.cp_r, refs.cq_s, refs.cq_r
+    x_sems = ((refs.x_s, refs.x_r), (refs.x2_s, refs.x2_r))
+    cp_sems = ((refs.cp_s, refs.cp_r), (refs.cp2_s, refs.cp2_r))
+    cq_sems = ((refs.cq_s, refs.cq_r), (refs.cq2_s, refs.cq2_r))
+    turn_sems = ((refs.turn_s, refs.turn_r), (refs.turn2_s, refs.turn2_r))
     block_r, gdown_r, tdown_r, prs_r = refs.block_r, refs.gdown_r, refs.tdown_r, refs.prs_r
     pqs_r, pair_s, pair_r, half_s = refs.pqs_r, refs.pair_s, refs.pair_r, refs.half_s
-    half_r, turn_s, turn_r = refs.half_r, refs.turn_s, refs.turn_r
+    half_r = refs.half_r
     p, q = lax.axis_index("row"), lax.axis_index("col")
     row_owner, col_owner, top_col = p == panel, q == panel, q == panel + 1
     core = lax.rem(p, 2)
@@ -403,13 +419,14 @@
 
     gather_row_start(pq_ref, pq_s, pq_r, p, q)
 
+    gather_col_wait(g_ref, whole, g_s, g_r, p, q)
+
     @pl.when(jnp.logical_not(col_owner))
     def _():
         pr_out(1).wait_recv()
 
     gather_col_start(pr_ref, piece, pr_s, pr_r, p, q)
 
-    gather_col_wait(g_ref, whole, g_s, g_r, p, q)
     kp_ref[...] = g_ref[...].reshape(B, B)
     chol_inverse(kp_ref, inv_ref, local.d_ref, local.half_ref, local.below_ref)
     gather_row_pass(pq_ref, pq_s, pq_r, p, q)
@@ -426,12 +443,12 @@
 
     lax.fori_loop(0, NS_STEPS, polar_step, 0)
     w = w_ref[...]
-    cross = dot(w, top, 0, 0)
-    metric = eye() + cross + cross.T + dot(w, w, 0, 0)
+    w_split = split(w)
+    cross = dot_split(w_split, split(top), 0, 0)
+    metric = eye() + cross + cross.T + dot_split(w_split, w_split, 0, 0)
     guess = (40.0 / 41.0) * eye() - (8.0 / 41.0) * metric
     for i in range(4):
-        mul = dot if i == 3 else dot3
-        guess = guess + mul(guess, eye() - mul(metric, guess, 1, 0), 1, 0)
+        guess = guess + dot3(guess, eye() - dot3(metric, guess, 1, 0), 1, 0)
     mid_ref[...] = 2.0 * guess
 
     gather_row_wait(pq_ref, pq_s, pq_r, p, q)
@@ -459,10 +476,14 @@
         vr_ref[:B, :] = vr_ref[:B, :] + w_ref[...]
 
     vq = split(vq_ref[...])
-    kp_ref[...] = jnp.zeros((B, B), jnp.float32)
-    x_out = lambda t: remote(
-        x_ref.at[piece(t)], parts.at[q], x_s.at[t], x_r.at[q], (p, t)
-    )
+    inner = [slice(0, PIECE // 2), slice(PIECE // 2, PIECE)]
+    within = [pl.ds(0, PIECE // 2), pl.ds(PIECE // 2, PIECE // 2)]
+
+    def x_out(t, h):
+        send, recv = x_sems[h]
+        return remote(
+            x_ref.at[HALVES[h](t)], parts.at[q, within[h]], send.at[t], recv.at[q], (p, t)
+        )
 
     def product_step(number, carry):
         tile = lax.rem(q // 4 + number, 4)
@@ -474,12 +495,14 @@
 
             @pl.when(t != q)
             def _():
-                x_out(t).start()
-
-        kp_ref[...] += dot3(vr_ref[rows, :], x, 0, 0)
+                x_out(t, 0).start()
+
         return carry
 
     lax.fori_loop(0, 4, product_step, 0)
+    for i in range(1, D):
+        x_out(col_peers[i], 1).start()
+    kp_ref[...] = dot3(vr_ref[...], x_ref[...], 0, 0)
     parts[q] = x_ref[piece(q), :]
     kp_out = lambda i: remote(
         kp_ref.at[slab(col_peers[i])], kparts.at[q], kp_s.at[i], kp_r.at[q], (p, col_peers[i])
@@ -492,25 +515,47 @@
         rows = slice(tile * B, tile * B + B)
         local.turned_vq[0][:, rows], local.turned_vq[1][:, rows] = split(vq_ref[rows, :].T)
 
-    for i in range(1, D):
-        t = col_peers[i]
-        remote(x_ref.at[piece(q)], parts.at[t], x_s.at[t], x_r.at[t], (p, t)).wait_recv()
-    total = parts[0]
-    for i in range(1, D):
-        total = total + parts[i]
-    image = dot(total, mid_ref[...], 1, 0)
-    cp_ref[piece(q), :] = image
-    turn_out = remote(cp_ref.at[piece(q)], cq_ref.at[piece(q)], turn_s, turn_r, (q, p))
-
-    @pl.when(p != q)
-    def _():
-        turn_out.start()
-
-    @pl.when(p == q)
-    def _():
-        cq_ref[piece(p), :] = image
-
-    gather_col_start(cp_ref, piece, cp_s, cp_r, p, q)
+    def turn_out(h):
+        send, recv = turn_sems[h]
+        return remote(cp_ref.at[HALVES[h](q)], cq_ref.at[HALVES[h](q)], send, recv, (q, p))
+
+    def turn_in(h):
+        send, recv = turn_sems[h]
+
+        @pl.when(p != q)
+        def _():
+            remote(
+                cp_ref.at[HALVES[h](q)], cq_ref.at[HALVES[h](p)], send, recv, (q, p)
+            ).wait_recv()
+
+        gather_row_start(cq_ref, *cq_sems[h], p, q, at=HALVES[h])
+
+    def image_half(h):
+        send, recv = x_sems[h]
+        for i in range(1, D):
+            t = col_peers[i]
+            remote(
+                x_ref.at[HALVES[h](q)], parts.at[t, within[h]], send.at[t], recv.at[t], (p, t)
+            ).wait_recv()
+        total = parts[0, inner[h]]
+        for i in range(1, D):
+            total = total + parts[i, inner[h]]
+        image = dot(total, mid_ref[...], 1, 0)
+        cp_ref[HALVES[h](q), :] = image
+
+        @pl.when(p != q)
+        def _():
+            turn_out(h).start()
+
+        @pl.when(p == q)
+        def _():
+            cq_ref[HALVES[h](p), :] = image
+
+        gather_col_start(cp_ref, HALVES[h], *cp_sems[h], p, q)
+
+    image_half(0)
+    image_half(1)
+    turn_in(0)
 
     for i in range(1, D):
         t = col_peers[i]
@@ -531,11 +576,7 @@
         kz_out(i).start()
     kz[p // 2] = khalf[mine, :]
 
-    @pl.when(p != q)
-    def _():
-        remote(cp_ref.at[piece(q)], cq_ref.at[piece(p)], turn_s, turn_r, (q, p)).wait_recv()
-
-    gather_row_start(cq_ref, cq_s, cq_r, p, q)
+    turn_in(1)
     for i in range(2, D, 2):
         t = row_peers[i] // 2
         remote(
@@ -558,19 +599,22 @@
 
             @pl.when(t != q)
             def _():
-                remote(
-                    cp_ref.at[piece(t)], cp_ref.at[piece(t)], cp_s.at[0], cp_r.at[t], (p, t)
-                ).wait_recv()
+                for at, (send, recv) in zip(HALVES, cp_sems):
+                    remote(
+                        cp_ref.at[at(t)], cp_ref.at[at(t)], send.at[0], recv.at[t], (p, t)
+                    ).wait_recv()
 
         subtract(a_vm, cp_ref, local.turned_vq, tile_rows(tile))
-        gather_row_pass(cq_ref, cq_s, cq_r, p, q, number)
+        for at, sems in zip(HALVES, cq_sems):
+            gather_row_pass(cq_ref, *sems, p, q, number, at=at)
     if panel == PANELS - 1:
         pltpu.make_async_copy(a_vm, local.a_out, local.store).start()
     gather_col_wait(k_ref, slab, k_s, k_r, p, q)
     middle = mid_ref[...]
     shift = dot3(dot3(middle, k_ref[...], 1, 0), middle, 1, 0)
     shift = split(0.5 * (shift + shift.T))
-    gather_row_wait(cq_ref, cq_s, cq_r, p, q)
+    for at, sems in zip(HALVES, cq_sems):
+        gather_row_wait(cq_ref, *sems, p, q, at=at)
     for tile in range(4):
         rows = slice(tile * B, tile * B + B)
         rest = cq_ref[rows, :] - dot_split(split(vq_ref[rows, :]), shift, 1, 0)
@@ -579,17 +623,20 @@
         subtract(a_vm, vr_ref, local.last, slice(0, B))
 
     def drain():
-        gather_row_drain(cq_ref, cq_s, cq_r, p, q)
+        for h in range(2):
+            gather_row_drain(cq_ref, *cq_sems[h], p, q, at=HALVES[h])
+            gather_col_drain(cp_ref, HALVES[h], *cp_sems[h], p, q)
         gather_row_drain(pq_ref, pq_s, pq_r, p, q)
         for ref, at, send, recv in (
-            (cp_ref, piece, cp_s, cp_r), (k_ref, slab, k_s, k_r), (pr_ref, piece, pr_s, pr_r),
+            (k_ref, slab, k_s, k_r), (pr_ref, piece, pr_s, pr_r),
             (g_ref, whole, g_s, g_r), (t_ref, whole, t_s, t_r),
         ):
             gather_col_drain(ref, at, send, recv, p, q)
 
         @pl.when(p != q)
         def _():
-            turn_out.wait_send()
+            turn_out(0).wait_send()
+            turn_out(1).wait_send()
 
         pair_out.wait_send()
         half_out.wait_send()
@@ -597,7 +644,8 @@
             kz_out(i).wait_send()
         for i in range(1, D):
             kp_out(i).wait_send()
-            x_out(col_peers[i]).wait_send()
+            x_out(col_peers[i], 0).wait_send()
+            x_out(col_peers[i], 1).wait_send()
 
         @pl.when(row_owner)
         def _():
@@ -652,7 +700,7 @@
 
 
 def finish(matrix, vr, high, low):
-    rows, size = 128, 4 * B
+    rows, size = B, 4 * B
     tile = lambda width: pl.BlockSpec((rows, width), lambda i: (i, 0))
     whole = pl.BlockSpec((B, size), lambda i: (0, 0))
     return pl.pallas_call(

time: 210 us -> 204 us (0.971)
  Pallas kernels: 207 us -> 203 us
    pallas_call x1, Pallas kernels: 199 us -> 197 us  [reduce_panels(): pl.pallas_call(reduce_kernel, out_shape=(jax.ShapeDtypeStruct((4 * B, 4 *...]
where the time goes in v4:
time: 204 us; the launch traced here: 203 us
  Pallas kernels  203 us (100%)
    pallas_call x1, Pallas kernels, reduce_panels(): pl.pallas_call(reduce_kernel, out_shape=(jax.ShapeDtypeStruct((4 * B, 4 *...  197 us
    pallas_call x1, Pallas kernels, finish(): pl.pallas_call(finish_kernel, out_shape=jax.ShapeDtypeStruct((size, size)...  6.38 us

profile of v4, /device:TPU:1, one launch (start us, length us, event | category | flops | bytes accessed | tf_op | source)
XLA Modules:
  0.0 203.4 jit_solution(13869294858910873315)
XLA Ops:
  0.0 197.0 %reduce_panels.1 = (f32[1024,1024]{1,0:T(8,128)}, f32[1024,256]{1,0:T(8,128)}, bf16[256,1024]{1,0:T(8,128)(2,1)}, bf16[256,1024]{1,0:T(8,128)(2,1)}) custom-call(f32[1024,1024]{1,0:T(8,128)} %a_ref.1), custom_call_target="tpu_custom_call" | custom-call | tf_op jit(solution)/shard_map/reduce_panels/pallas_call | solution.py:677
  197.1 6.4 %finish.1 = f32[1024,1024]{1,0:T(8,128)} custom-call(f32[1024,1024]{1,0:T(8,128)} %get-tuple-element.9.a_ref, f32[1024,256]{1,0:T(8,128)} %get-tuple-element.10.vr_ref, bf16[256,1024]{1,0:T(8,128)(2,1)} %get-tuple-element.11.high_ref, bf16[256,1024]{1,0:T(8,128)(2,1)} %get-tuple-element.12.low_ref), custom_call_target="tpu_custom_call" | custom-call | tf_op jit(solution)/shard_map/finish/pallas_call | solution.py:706

commit v5 on v4

--- a/solution.py
+++ b/solution.py
@@ -468,13 +468,6 @@
     def _():
         vq_ref[:B, :] = vq_ref[:B, :] + w
 
-    gather_col_wait(pr_ref, piece, pr_s, pr_r, p, q)
-    reflect(pr_ref, vr_ref)
-
-    @pl.when(p == panel + 1)
-    def _():
-        vr_ref[:B, :] = vr_ref[:B, :] + w_ref[...]
-
     vq = split(vq_ref[...])
     inner = [slice(0, PIECE // 2), slice(PIECE // 2, PIECE)]
     within = [pl.ds(0, PIECE // 2), pl.ds(PIECE // 2, PIECE // 2)]
@@ -502,6 +495,14 @@
     lax.fori_loop(0, 4, product_step, 0)
     for i in range(1, D):
         x_out(col_peers[i], 1).start()
+
+    gather_col_wait(pr_ref, piece, pr_s, pr_r, p, q)
+    reflect(pr_ref, vr_ref)
+
+    @pl.when(p == panel + 1)
+    def _():
+        vr_ref[:B, :] = vr_ref[:B, :] + w_ref[...]
+
     kp_ref[...] = dot3(vr_ref[...], x_ref[...], 0, 0)
     parts[q] = x_ref[piece(q), :]
     kp_out = lambda i: remote(

time: 204 us -> 202 us (level)
  no operation moved by 1% of the time
where the time goes in v5:
time: 202 us
  Pallas kernels  202 us (100%)
    pallas_call x1, Pallas kernels, reduce_panels(): pl.pallas_call(reduce_kernel, out_shape=(jax.ShapeDtypeStruct((4 * B, 4 *...  195 us
    pallas_call x1, Pallas kernels, finish(): pl.pallas_call(finish_kernel, out_shape=jax.ShapeDtypeStruct((size, size)...  6.38 us

profile of v5, /device:TPU:1, one launch (start us, length us, event | category | flops | bytes accessed | tf_op | source)
XLA Modules:
  0.0 201.8 jit_solution(1458205912823961518)
XLA Ops:
  0.0 195.4 %reduce_panels.1 = (f32[1024,1024]{1,0:T(8,128)}, f32[1024,256]{1,0:T(8,128)}, bf16[256,1024]{1,0:T(8,128)(2,1)}, bf16[256,1024]{1,0:T(8,128)(2,1)}) custom-call(f32[1024,1024]{1,0:T(8,128)} %a_ref.1), custom_call_target="tpu_custom_call" | custom-call | tf_op jit(solution)/shard_map/reduce_panels/pallas_call | solution.py:678
  195.4 6.4 %finish.1 = f32[1024,1024]{1,0:T(8,128)} custom-call(f32[1024,1024]{1,0:T(8,128)} %get-tuple-element.9.a_ref, f32[1024,256]{1,0:T(8,128)} %get-tuple-element.10.vr_ref, bf16[256,1024]{1,0:T(8,128)(2,1)} %get-tuple-element.11.high_ref, bf16[256,1024]{1,0:T(8,128)(2,1)} %get-tuple-element.12.low_ref), custom_call_target="tpu_custom_call" | custom-call | tf_op jit(solution)/shard_map/finish/pallas_call | solution.py:707

commit v6 on v5

--- a/solution.py
+++ b/solution.py
@@ -531,6 +531,8 @@
 
         gather_row_start(cq_ref, *cq_sems[h], p, q, at=HALVES[h])
 
+    middle_split = split(mid_ref[...])
+
     def image_half(h):
         send, recv = x_sems[h]
         for i in range(1, D):
@@ -541,7 +543,7 @@
         total = parts[0, inner[h]]
         for i in range(1, D):
             total = total + parts[i, inner[h]]
-        image = dot(total, mid_ref[...], 1, 0)
+        image = dot_split(split(total), middle_split, 1, 0)
         cp_ref[HALVES[h](q), :] = image
 
         @pl.when(p != q)

time: 202 us -> 201 us (level)
  no operation moved by 1% of the time
where the time goes in v6:
time: 201 us
  Pallas kernels  201 us (100%)
    pallas_call x1, Pallas kernels, reduce_panels(): pl.pallas_call(reduce_kernel, out_shape=(jax.ShapeDtypeStruct((4 * B, 4 *...  194 us
    pallas_call x1, Pallas kernels, finish(): pl.pallas_call(finish_kernel, out_shape=jax.ShapeDtypeStruct((size, size)...  6.38 us

profile of v6, /device:TPU:1, one launch (start us, length us, event | category | flops | bytes accessed | tf_op | source)
XLA Modules:
  0.0 200.9 jit_solution(68770520718305842)
XLA Ops:
  0.0 194.5 %reduce_panels.1 = (f32[1024,1024]{1,0:T(8,128)}, f32[1024,256]{1,0:T(8,128)}, bf16[256,1024]{1,0:T(8,128)(2,1)}, bf16[256,1024]{1,0:T(8,128)(2,1)}) custom-call(f32[1024,1024]{1,0:T(8,128)} %a_ref.1), custom_call_target="tpu_custom_call" | custom-call | tf_op jit(solution)/shard_map/reduce_panels/pallas_call | solution.py:680
  194.5 6.4 %finish.1 = f32[1024,1024]{1,0:T(8,128)} custom-call(f32[1024,1024]{1,0:T(8,128)} %get-tuple-element.9.a_ref, f32[1024,256]{1,0:T(8,128)} %get-tuple-element.10.vr_ref, bf16[256,1024]{1,0:T(8,128)(2,1)} %get-tuple-element.11.high_ref, bf16[256,1024]{1,0:T(8,128)(2,1)} %get-tuple-element.12.low_ref), custom_call_target="tpu_custom_call" | custom-call | tf_op jit(solution)/shard_map/finish/pallas_call | solution.py:709
